TPU v7x, 256 devices: a whole 4x4x8 slice. The times are simulated.
256 devices in a mesh: dp: 16 (over z, y_lo), seq: 16 (over x, y_hi, core).
Axes of the slice: x: 4, y: 4 (y_hi: 2, y_lo: 2; y = y_hi * 2 + y_lo), z: 8, core: 2. Of those that a mesh axis runs over, the one named last changes fastest.
Arguments:
- question_embedding_matrix: bfloat16 [512, 4096], P(('dp', 'seq'))
- passage_embedding_matrix: bfloat16 [512, 4096], P(('dp', 'seq'))
- positive: int32 [512], P(('dp', 'seq')), may hold values from 0 to 511
- queries: bfloat16 [16, 2048, 2048], P('dp', 'seq')
- keys: bfloat16 [16, 2048, 512], P('dp', 'seq')
- values: bfloat16 [16, 2048, 512], P('dp', 'seq'), may hold values from -6 to 6
- later_grad: bfloat16 [16, 2048, 2048], P('dp', 'seq'), may hold values from -6 to 6
- lengths: int32 [16], P('dp'), may hold values from 1 to 2048, 24576 in all
- q_gain: float32 [128], replicated, may hold values from 0.5 to 5
- k_gain: float32 [128], replicated, may hold values from 0.5 to 5
- out_weight: bfloat16 [2048, 4096], P('seq', 'dp'), may hold values from -0.09375 to 0.09375
Outputs:
- mean_loss: float32 [], replicated
- query_grad: bfloat16 [512, 4096], P(('dp', 'seq'))
- doc_grad: bfloat16 [512, 4096], P(('dp', 'seq'))
- query_cot: bfloat16 [16, 2048, 2048], P('dp', 'seq')
- key_cot: bfloat16 [16, 2048, 512], P('dp', 'seq')
- value_cot: bfloat16 [16, 2048, 512], P('dp', 'seq')
- q_gain_grad: float32 [128], replicated
- k_gain_grad: float32 [128], replicated
Inputs may be any that keep to these rules, and one draw needn't show every extreme that they name: `lengths`: every document has at least one valid token; the longest has exactly 2048.
All inputs are finite; a program needn't handle non-finite values. No bound on the sum of `lengths` on one device may be relied on, other than what follows from the above.
Results may differ from a plain program's by a relative error of at most 0.014.
The roundings to bfloat16 on the way count: a program that leaves them out, or rounds other values in their place, can miss the bound.
Values may be sent and summed in bfloat16 or wider, within the bound.
A program may use at most 128 MiB of HBM per device.

v0:
```python
import jax
import jax.numpy as jnp
from jax import lax
from jax.sharding import PartitionSpec as P

sharpness_divisor = 0.05
epsilon = 1e-06
rope_base = 1000000.0


def from_root(block, axis, source):
    block = jnp.where(lax.axis_index(axis) == source, block, jnp.zeros_like(block))
    return lax.psum(block, axis)


def rms_rope(inputs, gain, positions):
    head_dim = inputs.shape[-1]
    half_dim = head_dim // 2
    normed = inputs * lax.rsqrt(jnp.mean(inputs * inputs, axis=-1, keepdims=True) + epsilon) * gain
    frequency = rope_base ** (-2.0 * jnp.arange(half_dim, dtype=jnp.float32) / head_dim)
    angles = positions.astype(jnp.float32)[:, None] * frequency[None, :]
    cosine = jnp.cos(angles)[:, None, :]
    sine = jnp.sin(angles)[:, None, :]
    first_half = normed[..., :half_dim]
    second_half = normed[..., half_dim:]
    return jnp.concatenate(
        [first_half * cosine - second_half * sine, second_half * cosine + first_half * sine],
        axis=-1,
    )


def block_terms(query_rows, grad_rows, key_rows, value_rows, start_row, valid_len):
    block_rows = query_rows.shape[2]
    head_dim = query_rows.shape[3]
    scaling = head_dim ** (-0.5)
    col_index = jnp.arange(key_rows.shape[1])[None, :]
    row_index = start_row + jnp.arange(block_rows)[:, None]
    allowed = (col_index <= row_index) & (col_index < valid_len)
    scores = (
        jnp.einsum("kgtd,kud->kgtu", query_rows, key_rows, preferred_element_type=jnp.float32)
        * scaling
    )
    scores = jnp.where(allowed, scores, -1e30)
    highest = jnp.max(scores, axis=-1, keepdims=True)
    expon = jnp.exp(scores - highest)
    probs = expon / jnp.sum(expon, axis=-1, keepdims=True)
    probs_low = probs.astype(jnp.bfloat16)
    attn_out = jnp.einsum(
        "kgtu,kud->kgtd", probs_low, value_rows, preferred_element_type=jnp.float32
    )
    row_dot = jnp.sum(grad_rows.astype(jnp.float32) * attn_out, axis=-1, keepdims=True)
    value_part = jnp.einsum(
        "kgtu,kgtd->kud", probs_low, grad_rows, preferred_element_type=jnp.float32
    )
    prob_grad = jnp.einsum(
        "kgtd,kud->kgtu", grad_rows, value_rows, preferred_element_type=jnp.float32
    )
    score_grad = (probs * (prob_grad - row_dot) * scaling).astype(jnp.bfloat16)
    query_grad = jnp.einsum(
        "kgtu,kud->kgtd", score_grad, key_rows, preferred_element_type=jnp.float32
    )
    key_part = jnp.einsum(
        "kgtu,kgtd->kud", score_grad, query_rows, preferred_element_type=jnp.float32
    )
    return (query_grad, key_part, value_part)


def attend_blocks(query_block, key_block, value_block, grad_block, valid_len):
    groups, ratio, length, head_dim = query_block.shape
    block_rows = min(512, length)
    block_count = length // block_rows
    key_sum = jnp.zeros((groups, length, head_dim), jnp.float32)
    value_sum = jnp.zeros((groups, length, head_dim), jnp.float32)
    query_parts = []
    for block_index in range(block_count):
        start_row = block_index * block_rows
        end_row = start_row + block_rows
        operands = (
            query_block[:, :, start_row:end_row],
            grad_block[:, :, start_row:end_row],
            key_block[:, :end_row],
            value_block[:, :end_row],
        )

        def active_block(inputs, first=start_row):
            return block_terms(inputs[0], inputs[1], inputs[2], inputs[3], first, valid_len)

        def empty_block(inputs):
            return (
                jnp.zeros(inputs[0].shape, jnp.float32),
                jnp.zeros(inputs[2].shape, jnp.float32),
                jnp.zeros(inputs[3].shape, jnp.float32),
            )

        query_grad, key_part, value_part = lax.cond(
            start_row < valid_len, active_block, empty_block, operands
        )
        key_sum = key_sum.at[:, :end_row].add(key_part)
        value_sum = value_sum.at[:, :end_row].add(value_part)
        query_parts.append(query_grad)
    return (jnp.concatenate(query_parts, axis=2), key_sum, value_sum)


def shards(
    question_embedding_matrix,
    passage_embedding_matrix,
    positive,
    queries,
    keys,
    values,
    later_grad,
    lengths,
    q_gain,
    k_gain,
    out_weight,
):
    pair_dev = question_embedding_matrix.shape[0]
    pair_total = pair_dev * lax.axis_size(("dp", "seq"))
    gathered_documents = lax.all_gather(passage_embedding_matrix, ("dp", "seq"), axis=0, tiled=True)
    affinity_matrix = (
        jnp.dot(question_embedding_matrix, gathered_documents.T, preferred_element_type=jnp.float32)
        / sharpness_divisor
    )
    highest = jnp.max(affinity_matrix, axis=1, keepdims=True)
    normalizer_logsum = highest[:, 0] + jnp.log(jnp.sum(jnp.exp(affinity_matrix - highest), axis=1))
    positive_match_mask = (jnp.arange(pair_total)[None, :] == positive[:, None]).astype(jnp.float32)
    picked = jnp.sum(affinity_matrix * positive_match_mask, axis=1)
    loss_part = jnp.sum(normalizer_logsum - picked)
    normalized_affinity_shares = (
        (jnp.exp(affinity_matrix - normalizer_logsum[:, None]) - positive_match_mask)
        / sharpness_divisor
    ).astype(jnp.bfloat16)
    query_grad = jnp.dot(
        normalized_affinity_shares, gathered_documents, preferred_element_type=jnp.float32
    ).astype(jnp.bfloat16)
    doc_sum = lax.psum_scatter(
        jnp.dot(
            normalized_affinity_shares.T,
            question_embedding_matrix,
            preferred_element_type=jnp.float32,
        ),
        ("dp", "seq"),
        scatter_dimension=0,
        tiled=True,
    )
    doc_grad = doc_sum.astype(jnp.bfloat16)
    span_row = from_root(doc_grad[0:1], "seq", 0)
    tail = jnp.dot(
        span_row,
        lax.all_gather(out_weight, "dp", axis=1, tiled=True).T,
        preferred_element_type=jnp.float32,
    )
    tokens = queries.shape[1]
    head_dim = q_gain.shape[0]
    heads = queries.shape[2] // head_dim
    groups = keys.shape[2] // head_dim
    copies_count = max(1, lax.axis_size("seq") // groups)
    my_seq = lax.axis_index("seq")
    positions = my_seq * tokens + jnp.arange(tokens)

    def rope_at(inputs_in, gain):
        return rms_rope(inputs_in, gain, positions)

    q_rot, q_back = jax.vjp(
        rope_at, queries[0].reshape(tokens, heads, head_dim).astype(jnp.float32), q_gain
    )
    k_rot, k_back = jax.vjp(
        rope_at, keys[0].reshape(tokens, groups, head_dim).astype(jnp.float32), k_gain
    )
    q_send = q_rot.astype(jnp.bfloat16).reshape(1, tokens, heads * head_dim)
    k_send = k_rot.astype(jnp.bfloat16).reshape(1, tokens, groups * head_dim)
    q_heads, later_heads = (
        lax.all_to_all(q_send, "seq", split_axis=2, concat_axis=1, tiled=True),
        lax.all_to_all(later_grad, "seq", split_axis=2, concat_axis=1, tiled=True),
    )
    length = q_heads.shape[1]
    local_heads = q_heads.shape[2] // head_dim
    kv_stack = jnp.stack([k_send, values], 0)
    widened = jnp.broadcast_to(
        kv_stack.reshape(2, 1, tokens, groups, 1, head_dim),
        (2, 1, tokens, groups, copies_count, head_dim),
    )
    widened = widened.reshape(2, 1, tokens, groups * copies_count * head_dim)
    kv_heads = lax.all_to_all(widened, "seq", split_axis=3, concat_axis=2, tiled=True)
    local_groups = kv_heads.shape[3] // head_dim
    ratio = local_heads // local_groups
    query_block = q_heads[0].reshape(length, local_groups, ratio, head_dim).transpose(1, 2, 0, 3)
    key_block = kv_heads[0, 0].reshape(length, local_groups, head_dim).transpose(1, 0, 2)
    value_block = kv_heads[1, 0].reshape(length, local_groups, head_dim).transpose(1, 0, 2)
    valid_len = lengths[0]
    row_index = jnp.arange(length)[:, None]
    last_row = jnp.where(row_index == valid_len - 1, 1.0, 0.0)
    grad_rows = jnp.where(
        row_index < valid_len, later_heads[0].astype(jnp.float32) + last_row * tail, 0.0
    )
    grad_block = (
        grad_rows.astype(jnp.bfloat16)
        .reshape(length, local_groups, ratio, head_dim)
        .transpose(1, 2, 0, 3)
    )
    query_rgrad, key_rgrad, value_rgrad = attend_blocks(
        query_block, key_block, value_block, grad_block, valid_len
    )
    query_back = (
        query_rgrad.astype(jnp.bfloat16)
        .transpose(2, 0, 1, 3)
        .reshape(1, length, local_heads * head_dim)
    )
    query_tokens = lax.all_to_all(query_back, "seq", split_axis=1, concat_axis=2, tiled=True)
    kv_grads = (
        jnp.stack([key_rgrad, value_rgrad], 0)
        .transpose(0, 2, 1, 3)
        .reshape(2, 1, length, local_groups * head_dim)
    )
    returned = lax.all_to_all(kv_grads, "seq", split_axis=2, concat_axis=3, tiled=True)
    returned = returned.reshape(2, 1, tokens, groups, copies_count, head_dim).sum(axis=4)
    returned = returned.reshape(2, 1, tokens, groups * head_dim)
    query_low = lax.optimization_barrier(query_tokens[0])
    key_low = lax.optimization_barrier(returned[0, 0].astype(jnp.bfloat16))
    query_in, q_gain_part = q_back(query_low.astype(jnp.float32).reshape(tokens, heads, head_dim))
    key_in, k_gain_part = k_back(key_low.astype(jnp.float32).reshape(tokens, groups, head_dim))
    query_cot = query_in.reshape(1, tokens, heads * head_dim).astype(jnp.bfloat16)
    key_cot = key_in.reshape(1, tokens, groups * head_dim).astype(jnp.bfloat16)
    value_cot = returned[1].astype(jnp.bfloat16)
    loss_total, q_gain_grad, k_gain_grad = lax.psum(
        (loss_part, q_gain_part, k_gain_part), ("dp", "seq")
    )
    return (
        loss_total / pair_total,
        query_grad,
        doc_grad,
        query_cot,
        key_cot,
        value_cot,
        q_gain_grad,
        k_gain_grad,
    )


def solution(mesh):
    in_specs = (
        P(("dp", "seq"), None),
        P(("dp", "seq"), None),
        P(("dp", "seq")),
        P("dp", "seq", None),
        P("dp", "seq", None),
        P("dp", "seq", None),
        P("dp", "seq", None),
        P("dp"),
        P(),
        P(),
        P("seq", "dp"),
    )
    out_specs = (
        P(),
        P(("dp", "seq"), None),
        P(("dp", "seq"), None),
        P("dp", "seq", None),
        P("dp", "seq", None),
        P("dp", "seq", None),
        P(),
        P(),
    )
    return jax.shard_map(shards, mesh=mesh, in_specs=in_specs, out_specs=out_specs, check_vma=False)
```

profile of v0, /device:TPU:1, one launch (start us, length us, event | category | flops | bytes accessed | tf_op | source)
XLA Modules:
  0.0 843.7 jit_solution(11420632068910051686)
XLA Ops:
  11.2 8.1 copy.193
  19.9 11.5 %reduce.46 = bf16[2048,128]{1,0:T(8,128)(2,1)S(1)} reduce(bf16[2048,1,128]{2,1,0:T(2,128)(2,1)S(1)} %bitcast.239, bf16[]{:T(256)} %broadcast.553), dimensions={1}, to_apply=%bitcast.220.reduce_sub_computation | reduce | bytes 1048578
  32.3 8.7 %all-to-all-start = ((bf16[16,2,8192]{2,1,0:T(2,128)(2,1)}), bf16[16,2,8192]{2,1,0:T(2,128)(2,1)S(1)}, u32[]{:S(2)}, u32[]{:S(2)}) async-start(bf16[16,2,8192]{2,1,0:T(2,128)(2,1)} %reshape.969), calls=%async_computation | async-start | bytes 1048576 | tf_op jit(solution)/shard_map/all_to_all | solution.py:173
  43.1 2.4 copy.158
  45.5 11.5 %reduce.47 = bf16[2048,128]{1,0:T(8,128)(2,1)S(1)} reduce(bf16[2048,1,128]{2,1,0:T(2,128)(2,1)S(1)} %bitcast.243, bf16[]{:T(256)} %broadcast.553), dimensions={1}, to_apply=%bitcast.180.reduce_sub_computation | reduce | bytes 1048578
  58.0 7.2 all-to-all-start.2
  67.6 8.9 %all-to-all-done.2 = bf16[16,2,8192]{2,1,0:T(2,128)(2,1)S(1)} async-done(((bf16[16,2,8192]{2,1,0:T(2,128)(2,1)}), bf16[16,2,8192]{2,1,0:T(2,128)(2,1)S(1)}, u32[]{:S(2)}, u32[]{:S(2)}) %all-to-all-start.2) | async-done | bytes 524320 | tf_op jit(solution)/shard_map/all_to_all | solution.py:174
  76.5 1.8 broadcast_in_dim.63
  78.3 4.3 all-to-all-start.1
  85.2 2.2 reshape.970
  88.3 2.0 copy.150
  90.3 2.2 reshape.972
  95.5 4.2 all-to-all-done.1
  101.3 327.7 %all-gather.6.cloned.1.call-done = bf16[256,2,4096]{2,1,0:T(2,128)(2,1)} async-done(((bf16[1,2,4096]{2,1,0:T(2,128)(2,1)}), bf16[256,2,4096]{2,1,0:T(2,128)(2,1)}) %all-gather.6.cloned.1.call-update) | async-done | bytes 4194320 | tf_op jit(solution)/shard_map/all_gather | solution.py:119
  429.0 7.2 reshape.965
  436.2 3.5 fusion.117
  441.0 4.6 fusion.109
  445.6 153.0 %all-reduce.9 = bf16[512,4096]{1,0:T(8,128)(2,1)} all-reduce(f32[512,4096]{1,0:T(8,128)} %fusion.109), channel_id=2, replica_groups=mesh['dp'=16,'seq'=16] {'dp','seq'}, use_global_device_ids=true, to_apply=%region_5.6.clone | all-reduce | flops 2097152 | bytes 12582912
  600.1 34.4 %psum.29 = bf16[4096]{0:T(1024)(128)(2,1)S(1)} all-reduce(bf16[4096]{0:T(1024)(128)(2,1)S(1)} %fusion.105), channel_id=1, replica_groups=mesh['dp'=16,'seq'=16] {'seq'}, use_global_device_ids=true, to_apply=%region_8.9 | all-reduce | flops 4096 | bytes 16384 | tf_op jit(solution)/shard_map/psum | solution.py:13
  634.6 1.6 convolution_bitcast_fusion.12
  637.1 6.0 conditional.4
  637.8 1.3 fusion.110
  645.0 2.0 scatter-add.25
  647.0 7.2 conditional.5
  647.8 1.8 fusion.111
  652.6 1.4 convolution_bitcast_fusion.4
  655.3 8.7 %conditional.6 = (f32[1,1536,128]{2,1,0:T(8,128)S(1)}, f32[1,1536,128]{2,1,0:T(8,128)S(1)}, bf16[1,512,128]{2,0,1:T(2,128)(2,1)S(1)}) conditional(s32[]{:T(128)} %convert_element_type.224, () %tuple.111, (s32[]{:T(128)}, bf16[1,1,2048,128]{3,2,1,0:T(8,128)(2,1)}, bf16[1,2048,128]{2,1,0:T(8,128)(2,1)}, bf16[1,1,2048,128]{2,3,1,0:T(8,128)(2,1)S(1)}, ...), branch_computations={%region_19.20_spmd, %region_20.24_spmd} | conditional | flops 1220018688 | bytes 33051704 | solution.py:95
  656.0 2.1 fusion.112
  662.3 1.5 convolution_bitcast_fusion.7
  665.2 9.6 %conditional.7 = (f32[1,2048,128]{2,1,0:T(8,128)}, f32[1,2048,128]{2,1,0:T(8,128)}, bf16[1,512,128]{2,0,1:T(2,128)(2,1)S(1)}) conditional(s32[]{:T(128)} %convert_element_type.225, () %tuple.112, (s32[]{:T(128)}, bf16[1,1,2048,128]{3,2,1,0:T(8,128)(2,1)}, bf16[1,2048,128]{2,1,0:T(8,128)(2,1)}, bf16[1,1,2048,128]{2,3,1,0:T(8,128)(2,1)S(1)}, ...), branch_computations={%region_24.25_spmd, %region_25.29_spmd} | conditional | flops 1626604544 | bytes 43014200 | solution.py:95
  674.9 8.0 fusion.118
  682.9 12.6 %reduce.48 = bf16[2048,128]{1,0:T(8,128)(2,1)S(1)} reduce(bf16[2048,1,128]{2,1,0:T(2,128)(2,1)} %fusion.118, bf16[]{:T(256)} %broadcast.553), dimensions={1}, to_apply=%fusion.118.reduce_sub_computation | reduce | bytes 1048578
  696.4 5.4 all-to-all-start.3
  701.8 1.9 add_dynamic-update-slice_fusion
  704.8 2.7 fusion.100
  707.6 1.6 add.177
  709.2 1.3 add.174
  710.5 3.0 pad_maximum_fusion
  714.4 7.7 all-to-all-start.4
  722.1 3.5 convolution_convert_fusion.4
  725.6 3.5 reshape.974
  729.1 2.1 copy.186
  731.2 2.0 copy.165
  735.4 1.5 multiply_reduce_fusion
  738.0 2.0 copy.173
  740.1 10.3 %all-to-all-done.4 = f32[2,1,2048,128]{3,1,0,2:T(1,128)S(1)} async-done(((f32[2,1,2048,128]{3,1,0,2:T(1,128)}), f32[2,1,2048,128]{3,1,0,2:T(1,128)S(1)}, u32[]{:S(2)}, u32[]{:S(2)}) %all-to-all-start.4) | async-done | bytes 2097184 | tf_op jit(solution)/shard_map/all_to_all | solution.py:215
  750.4 1.3 reduce.43
  756.1 78.4 %all-reduce.7 = (f32[]{:T(128)}, f32[128]{0:T(128)}, f32[128]{0:T(128)}) all-reduce(f32[]{:T(128)} %get-tuple-element.312, f32[128]{0:T(128)S(1)} %copy-done.39, f32[128]{0:T(128)S(1)} %get-tuple-element.305), channel_id=1, replica_groups=mesh['dp'=16,'seq'=16] {'dp','seq'}, use_global_device_ids=true, to_apply=%region_4.0 | all-reduce | flops 257 | bytes 2056 | tf_op jit(solution)/shard_map/psum | solution.py:225
  (177 shorter events, 51.9 us)
Async XLA Ops:
  7.2 429.0 %copy-start = (bf16[2,4096]{1,0:T(2,128)(2,1)S(1)}, bf16[2,4096]{1,0:T(2,128)(2,1)}, u32[]{:S(2)}) copy-start(bf16[2,4096]{1,0:T(2,128)(2,1)} %param.39) | copy-start | bytes 49156
  7.2 421.8 %all-gather.6.cloned.1.call-start = ((), (), s32[]{:S(2)}) async-start(), calls=%async_computation.6 | async-start | bytes 4210688 | tf_op jit(solution)/shard_map/all_gather | solution.py:119
  9.3 0.6 copy-start.28
  9.9 1.1 copy-start.22
  10.1 31.0 %copy-start.19 = (f32[128,64]{0,1:T(8,128)}, f32[128,64]{0,1:T(8,128)S(1)}, u32[]{:S(2)}) copy-start(f32[128,64]{0,1:T(8,128)S(1)} %get-tuple-element.336) | copy-start | bytes 98308
  10.1 31.1 %copy-start.20 = (f32[128,64]{0,1:T(8,128)}, f32[128,64]{0,1:T(8,128)S(1)}, u32[]{:S(2)}) copy-start(f32[128,64]{0,1:T(8,128)S(1)} %get-tuple-element.337) | copy-start | bytes 98308
  11.1 30.8 %copy-start.25 = (bf16[1,128,512]{2,1,0:T(8,128)(2,1)S(1)}, bf16[1,128,512]{2,1,0:T(8,128)(2,1)}, u32[]{:S(2)}) copy-start(bf16[1,128,512]{2,1,0:T(8,128)(2,1)} %param.44) | copy-start | bytes 393220
  11.2 31.5 %copy-start.24 = (bf16[1,128,512]{2,1,0:T(8,128)(2,1)S(1)}, bf16[1,128,512]{2,1,0:T(8,128)(2,1)}, u32[]{:S(2)}) copy-start(bf16[1,128,512]{2,1,0:T(8,128)(2,1)} %param.43) | copy-start | bytes 393220
  32.3 25.6 %all-to-all-start = ((bf16[16,2,8192]{2,1,0:T(2,128)(2,1)}), bf16[16,2,8192]{2,1,0:T(2,128)(2,1)S(1)}, u32[]{:S(2)}, u32[]{:S(2)}) async-start(bf16[16,2,8192]{2,1,0:T(2,128)(2,1)} %reshape.969), calls=%async_computation | async-start | bytes 1048576 | tf_op jit(solution)/shard_map/all_to_all | solution.py:173
  43.0 2.5 copy-start.31
  57.0 10.1 %copy-start.21 = (bf16[1,1,128,4,1,128]{5,3,2,4,1,0:T(4,128)(2,1)S(1)}, bf16[1,1,128,4,1,128]{5,3,2,4,1,0:T(4,128)(2,1)}, u32[]{:S(2)}) copy-start(bf16[1,1,128,4,1,128]{5,3,2,4,1,0:T(4,128)(2,1)} %stack.15) | copy-start | bytes 393220
  58.0 20.4 %copy-start.8 = (bf16[16,2,8192]{2,1,0:T(2,128)(2,1)}, bf16[16,2,8192]{2,1,0:T(2,128)(2,1)S(1)}, u32[]{:S(2)}) copy-start(bf16[16,2,8192]{2,1,0:T(2,128)(2,1)S(1)} %all-to-all-done) | copy-start | bytes 1572868
  58.0 18.6 %all-to-all-start.2 = ((bf16[16,2,8192]{2,1,0:T(2,128)(2,1)}), bf16[16,2,8192]{2,1,0:T(2,128)(2,1)S(1)}, u32[]{:S(2)}, u32[]{:S(2)}) async-start(bf16[16,2,8192]{2,1,0:T(2,128)(2,1)} %reshape.971), calls=%async_computation.2 | async-start | bytes 1048576 | tf_op jit(solution)/shard_map/all_to_all | solution.py:174
  76.5 1.8 copy-start.9
  78.3 21.4 %all-to-all-start.1 = ((bf16[2,1,128,2048]{2,0,1,3:T(2,128)(2,1)}), bf16[2,1,128,2048]{2,0,1,3:T(2,128)(2,1)S(1)}, u32[]{:S(2)}, u32[]{:S(2)}) async-start(bf16[2,1,128,2048]{2,0,1,3:T(2,128)(2,1)} %bitcast.41), calls=%async_computation.1 | async-start | bytes 2097152 | tf_op jit(solution)/shard_map/all_to_all | solution.py:184
  82.6 552.0 %all-gather.4.cloned.1.call-start = ((), (), s32[]{:S(2)}) async-start(), calls=%async_computation.5 | async-start | bytes 1114112 | tf_op jit(solution)/shard_map/all_gather | solution.py:150
  436.2 3.5 copy-start.33
  439.7 0.9 copy-start.26
  440.5 0.5 copy-start.35
  445.6 190.6 %copy-start.2 = (f32[1,1,2048,128]{2,3,1,0:T(8,128)S(1)}, f32[1,1,2048,128]{2,3,1,0:T(8,128)}, u32[]{:S(2)}) copy-start(f32[1,1,2048,128]{2,3,1,0:T(8,128)} %reshape.958) | copy-start | bytes 3145732
  599.5 0.6 copy-start.30
  643.1 0.7 copy-start.14
  643.1 0.8 copy-start.15
  643.1 0.9 copy-start.16
  651.1 1.0 copy-start.3
  654.2 0.8 copy-start.13
  654.2 0.9 copy-start.17
  654.2 1.1 copy-start.11
  660.6 1.0 copy-start.4
  664.0 0.9 copy-start.6
  664.0 1.2 copy-start.7
  664.0 1.2 copy-start.18
  674.9 26.9 %copy-start.12 = (f32[1,1024,128]{2,1,0:T(8,128)S(1)}, f32[1,1024,128]{2,1,0:T(8,128)}, u32[]{:S(2)}) copy-start(f32[1,1024,128]{2,1,0:T(8,128)} %copy-done.11) | copy-start | bytes 1572868
  696.4 17.2 %all-to-all-start.3 = ((bf16[16,2,8192]{2,1,0:T(2,128)(2,1)}), bf16[16,2,8192]{2,1,0:T(2,128)(2,1)S(1)}, u32[]{:S(2)}, u32[]{:S(2)}) async-start(bf16[16,2,8192]{2,1,0:T(2,128)(2,1)} %reshape.973), calls=%async_computation.3 | async-start | bytes 1048576 | tf_op jit(solution)/shard_map/all_to_all | solution.py:209
  713.6 8.5 %copy-start.27 = (f32[2,512]{1,0:T(2,128)S(1)}, f32[2,512]{1,0:T(2,128)}, u32[]{:S(2)}) copy-start(f32[2,512]{1,0:T(2,128)} %copy-done.26) | copy-start | bytes 12292
  713.6 8.5 %copy-start.34 = (s32[2]{0:T(128)S(1)}, s32[2]{0:T(128)}, u32[]{:S(2)}) copy-start(s32[2]{0:T(128)} %param.41) | copy-start | bytes 28
  713.6 8.5 %copy-start.36 = (f32[2]{0:T(128)S(1)}, f32[2]{0:T(128)}, u32[]{:S(2)}) copy-start(f32[2]{0:T(128)} %copy-done.35) | copy-start | bytes 28
  713.6 0.8 copy-start.10
  714.4 36.0 %all-to-all-start.4 = ((f32[2,1,2048,128]{3,1,0,2:T(1,128)}), f32[2,1,2048,128]{3,1,0,2:T(1,128)S(1)}, u32[]{:S(2)}, u32[]{:S(2)}) async-start(f32[2,1,2048,128]{3,1,0,2:T(1,128)} %pad_maximum_fusion), calls=%async_computation.4 | async-start | bytes 4194304 | tf_op jit(solution)/shard_map/all_to_all | solution.py:215
  729.1 6.3 copy-start.23
  733.2 3.7 copy-start.29
  733.2 3.7 copy-start.38
  751.7 2.5 copy-start.37
  751.7 3.1 copy-start.32
  751.7 83.4 %copy-start.1 = (bf16[2,4096]{1,0:T(2,128)(2,1)S(1)}, bf16[2,4096]{1,0:T(2,128)(2,1)}, u32[]{:S(2)}) copy-start(bf16[2,4096]{1,0:T(2,128)(2,1)} %param.39) | copy-start | bytes 49156
  751.8 4.3 copy-start.39
Sparse Core Ops, SparseCore 0:
  9.9 419.0 all-gather.5
  430.7 61.9 all-gather.3
where the time goes:
time: 853 us; the launch traced here: 844 us
  waiting for transfers between devices  352 us (41%)
  blocking collectives  266 us (31%)
  other arithmetic  75.9 us (9%)
  local copies, waits for them, and re-layouts  61.3 us (7%)
  starting transfers between devices  33.8 us (4%)
  matrix products  29.3 us (3%)
  between operations  17.7 us (2%)
    all_gather x1, waiting for transfers between devices, shards(): lax.all_gather(passage_embedding_matrix, ('dp', 'seq'), axis=0, tiled=True)  328 us
    unnamed x1, blocking collectives  153 us
    psum x1, blocking collectives, shards(): lax.psum((loss_part, q_gain_part, k_gain_part), ('dp', 'seq'))  78.4 us
    unnamed x5, other arithmetic  44.9 us
    psum x1, blocking collectives, from_root(): return lax.psum(block, axis)  34.4 us
    unnamed x90, local copies, waits for them, and re-layouts  32.5 us
  transfers between devices with their start and end apart: 7, of which 4 were waited for; matrix products, arithmetic and copies ran while one was open for 12% of the time, Pallas kernels for 0%

commit v1 on v0

v1 whole, which is shorter than its diff:
```python
import functools
import math

import jax
import jax.numpy as jnp
from jax import lax
from jax.experimental import pallas as pl
from jax.experimental.pallas import tpu as pltpu
from jax.sharding import PartitionSpec as P

sharpness = 0.05
epsilon = 1e-06
rope_base = 1000000.0
lowest = -1e30
MESH = pl.DeviceIdType.MESH
f32 = jnp.float32
bf16 = jnp.bfloat16
VMEM = pl.BlockSpec(memory_space=pltpu.VMEM)
limit = 58 * 1024 * 1024
count = 16
pairs = 32
chunks = 32
q_stride = 40
scaling = 128 ** (-0.5)
phases = (
    "q_msg", "p_msg", "tile", "part", "span", "tail_part", "q_term", "d_term", "gain_seq",
    "gain_dp", "kv_x", "kv_y", "kv_core", "kv_both", "q", "grad", "dq", "core_sum", "y_sum",
    "x_out", "tail",
)
phase_of = {name: i for i, name in enumerate(phases)}


def mm(a, b):
    return lax.dot_general(a, b, (((1,), (0,)), ((), ())), preferred_element_type=f32)


def mm_nt(a, b):
    return lax.dot_general(a, b, (((1,), (1,)), ((), ())), preferred_element_type=f32)


def mm_tn(a, b):
    return lax.dot_general(a, b, (((0,), (0,)), ((), ())), preferred_element_type=f32)


def loop(first, last, step):
    def body(i, carry):
        step(i)
        return carry

    lax.fori_loop(first, last, body, 0)


def swap_halves(x):
    return pltpu.roll(x, 64, 1)


def normed_rope(x, gain, cosine, sine):
    scale = lax.rsqrt(jnp.mean(x * x, axis=-1, keepdims=True) + epsilon)
    y = x * scale * gain
    return y * cosine + swap_halves(y) * sine


def normed_rope_back(x, gain, cosine, sine, grad):
    scale = lax.rsqrt(jnp.mean(x * x, axis=-1, keepdims=True) + epsilon)
    n = x * scale
    dy = grad * cosine - swap_halves(grad) * sine
    gain_part = dy * n
    dn = dy * gain
    dx = scale * (dn - n * jnp.mean(dn * n, axis=-1, keepdims=True))
    return dx, gain_part


def slot_sum(ref):
    total = ref[0]
    for i in range(1, count):
        total = total + ref[i]
    return total


def whole(
    lengths, queries, keys, values, later, q_emb, p_emb, pos_hi, pos_lo, out_w, q_gain, k_gain,
    cosine, sine,
    loss_out, q_grad_out, d_grad_out, q_cot, k_cot, v_cot, gains_out,
    q_f32, q_msg, p_f32, p_msg, q_all, p_all, q_wide, p_wide, q_cols, p_cols, q_part, tiles,
    w_span, q_terms, d_terms, q_slots, d_slots, tail_slots, tail_send, tail_in,
    kv_stage, q_stage, grad_stage, kv_h, q_h, grad_h,
    scores, prob_grads, shares, dq_acc, dkv, dq_stage, dq_slots,
    core_slots, y_stage, y_slots, x_stage, x_slots, seq_slots, dp_slots,
    send_sem, recv_sem,
):
    d, j = lax.axis_index("dp"), lax.axis_index("seq")
    x, y, c = j // 4, (j // 2) % 2, j % 2
    rank = 2 * x + c
    barrier = pltpu.get_barrier_semaphore()

    def remote(name, src, dst, to_slot, from_slot, dp, seq):
        phase = phase_of[name]
        return pltpu.make_async_remote_copy(
            src_ref=src,
            dst_ref=dst,
            send_sem=send_sem.at[phase, to_slot],
            recv_sem=recv_sem.at[phase, from_slot],
            device_id=(dp, seq),
            device_id_type=MESH,
        )

    def others(step, me, size=count):
        loop(1, size, lambda o: step(lax.rem(me + o, size)))

    class Axis:
        def __init__(self, name, axis, src, dst):
            self.name, self.src, self.dst = name, src, dst
            self.me = d if axis == "dp" else j
            self.place = (lambda p: (p, j)) if axis == "dp" else (lambda p: (d, p))

        def send(self):
            others(
                lambda p: remote(
                    self.name, self.src(p), self.dst(self.me), p, self.me, *self.place(p)
                ).start(),
                self.me,
            )

        def arrive(self):
            others(
                lambda p: remote(
                    self.name, self.src(p), self.dst(p), p, p, *self.place(p)
                ).wait_recv(),
                self.me,
            )

        def sent(self):
            others(
                lambda p: remote(
                    self.name, self.src(p), self.dst(self.me), p, self.me, *self.place(p)
                ).wait_send(),
                self.me,
            )

    others(
        lambda p: pl.semaphore_signal(barrier, inc=1, device_id=(d, p), device_id_type=MESH), j
    )
    others(
        lambda p: pl.semaphore_signal(barrier, inc=1, device_id=(p, j), device_id_type=MESH), d
    )

    def lanes(h):
        return pl.ds(pl.multiple_of(h * 128, 128), 128)

    def q_rows(s):
        return pl.ds(pl.multiple_of(s * 2 * q_stride, 16), 2 * q_stride)

    def p_rows(s):
        return pl.ds(pl.multiple_of(s * 2 * chunks, 16), 2 * chunks)

    q_f32[...] = jnp.zeros_like(q_f32)
    q_own, p_own = q_emb[...].astype(f32), p_emb[...].astype(f32)
    for i in range(chunks):
        q_f32[pl.ds(i, 2, stride=q_stride), :] = q_own[:, i * 128 : i * 128 + 128]
        p_f32[pl.ds(i, 2, stride=chunks), :] = p_own[:, i * 128 : i * 128 + 128]
    q_f32[pl.ds(chunks, 2, stride=q_stride), :] = pos_hi[...]
    q_f32[pl.ds(chunks + 1, 2, stride=q_stride), :] = pos_lo[...]
    q_msg[...] = q_f32[...].astype(bf16)
    p_msg[...] = p_f32[...].astype(bf16)
    q_all[q_rows(j), :] = q_msg[...]
    p_all[p_rows(d), :] = p_msg[...]

    def stage_kv(g):
        rot = normed_rope(keys[:, lanes(g)].astype(f32), k_gain[...], cosine[...], sine[...])
        kv_stage[g, 0] = rot.astype(bf16)
        kv_stage[g, 1] = values[:, lanes(g)]

    loop(0, 4, stage_kv)
    pl.semaphore_wait(barrier, 2 * (count - 1))

    q_x = Axis("q_msg", "seq", lambda p: q_msg, lambda s: q_all.at[q_rows(s)])
    p_x = Axis("p_msg", "dp", lambda p: p_msg, lambda s: p_all.at[p_rows(s)])
    q_x.send()
    p_x.send()

    def kv_spot(a, b, e):
        return kv_h.at[:, a, b, e]

    def kv_x(to, source):
        return remote("kv_x", kv_stage.at[to], kv_spot(source, y, c), to, source, d, 4 * to + 2 * y + c)

    others(lambda p: kv_x(p, x).start(), x, 4)
    kv_h[:, x, y, c] = kv_stage[x]

    def kv_pass(name, a, b, e, seq):
        return remote(name, kv_spot(a, b, e), kv_spot(a, b, e), a, a, d, seq)

    over_y = 4 * x + 2 * (1 - y) + c
    over_core = 4 * x + 2 * y + (1 - c)

    def pass_on(a):
        kv_pass("kv_y", a, y, c, over_y).start()
        kv_pass("kv_core", a, y, c, over_core).start()

    pass_on(x)

    def stage_q(h):
        rot = normed_rope(queries[:, lanes(h)].astype(f32), q_gain[...], cosine[...], sine[...])
        q_stage[h // 2, h % 2] = rot.astype(bf16)

    def seat(r):
        return 4 * (r // 2) + 2 * y + r % 2

    def head_copy(name, stage, held, to, source):
        return remote(
            name, stage.at[to], held.at[source // 2, :, source % 2], to, source, d, seat(to)
        )

    loop(0, 16, stage_q)
    others(lambda p: head_copy("q", q_stage, q_h, p, rank).start(), rank, 8)
    q_h[x, :, c] = q_stage[rank]

    def stage_grad(h):
        grad_stage[h // 2, h % 2] = later[:, lanes(h)]

    loop(0, 16, stage_grad)
    others(lambda p: head_copy("grad", grad_stage, grad_h, p, rank).start(), rank, 8)
    grad_h[x, :, c] = grad_stage[rank]
    dkv[...] = jnp.zeros_like(dkv)

    q_x.arrive()
    p_x.arrive()
    q_wide[...] = q_all[...].astype(f32)
    p_wide[...] = p_all[...].astype(f32)
    for i in range(chunks):
        half = pl.ds((i % 2) * 128, 128)
        q_cols[i // 2, :, half] = q_wide[pl.ds(i, pairs, stride=q_stride), :].astype(bf16)
        p_cols[i // 2, :, half] = p_wide[pl.ds(i, pairs, stride=chunks), :].astype(bf16)
    positive = (
        2.0 * q_wide[pl.ds(chunks, pairs, stride=q_stride), :]
        + q_wide[pl.ds(chunks + 1, pairs, stride=q_stride), :]
    )
    q_part[d] = q_cols[d]
    part_x = Axis("part", "dp", lambda p: q_cols.at[p], lambda s: q_part.at[s])
    part_x.send()

    def four(block):
        return jnp.concatenate([block] * (128 // pairs), axis=0)

    logits = mm_nt(q_cols[0], four(p_cols[0]))
    for b in range(1, count):
        logits = logits + mm_nt(q_cols[b], four(p_cols[b]))
    logits = logits / sharpness
    lane = lax.broadcasted_iota(jnp.int32, (pairs, 128), 1)
    real = lane < pairs
    base = jnp.where(real, (lane >> 1) * pairs + (lane & 1), -(1 << 20)).astype(f32)
    tiles[j] = jnp.where(real, logits, lowest)
    tile_x = Axis("tile", "seq", lambda p: tiles.at[j], lambda s: tiles.at[s])
    tile_x.send()

    def pass_arrived(a):
        kv_x(a, a).wait_recv()
        pass_on(a)

    others(pass_arrived, x, 4)

    tile_x.arrive()
    high = tiles[0]
    for i in range(1, count):
        high = jnp.maximum(high, tiles[i])
    high = jnp.max(high, axis=1, keepdims=True)
    mass = jnp.zeros((pairs, 128), f32)
    hit = jnp.zeros((pairs, 128), f32)
    for i in range(count):
        mass = mass + jnp.exp(tiles[i] - high)
        hit = hit + jnp.where(base + 2.0 * i == positive, tiles[i], 0.0)
    log_total = high + jnp.log(jnp.sum(mass, axis=1, keepdims=True))
    picked = jnp.sum(hit, axis=1, keepdims=True)
    loss_part = jnp.sum(log_total - picked, axis=0, keepdims=True)

    def weights_of(tile, index):
        onehot = jnp.where(base + 2.0 * index == positive, 1.0, 0.0)
        return (jnp.exp(tile - log_total) - onehot) / sharpness

    w_span[d] = weights_of(tiles[0], 0.0).astype(bf16)
    span_x = Axis("span", "dp", lambda p: w_span.at[d], lambda s: w_span.at[s])
    span_x.send()
    mine = weights_of(tiles[j], j.astype(f32))
    w = mine.astype(bf16)
    w_t = jnp.transpose(mine)[:pairs].astype(bf16)

    def pass_from_y(o):
        a = lax.rem(x + o, 4)
        kv_pass("kv_y", a, 1 - y, c, over_y).wait_recv()
        kv_pass("kv_both", a, 1 - y, c, over_core).start()

    loop(0, 4, pass_from_y)

    part_x.arrive()
    span_x.arrive()
    span = mm_tn(w_span[...].reshape(pairs * count, 128), q_part[...].reshape(pairs * count, 256))
    span = span[:pairs].astype(bf16)
    tail_slots[d, pl.ds(0, pairs)] = mm_nt(span, out_w[...])
    tail_slots[d, pl.ds(pairs, 8)] = jnp.broadcast_to(loss_part, (8, 128))
    tail_x = Axis("tail_part", "dp", lambda p: tail_slots.at[d], lambda s: tail_slots.at[s])
    tail_x.send()

    def kv_core_arrive(a):
        kv_pass("kv_core", a, y, 1 - c, over_core).wait_recv()
        kv_pass("kv_both", a, 1 - y, 1 - c, over_core).wait_recv()

    loop(0, 4, kv_core_arrive)
    others(lambda p: head_copy("q", q_stage, q_h, p, p).wait_recv(), rank, 8)
    length = lengths[0]
    key_spot = lax.broadcasted_iota(jnp.int32, (512, 512), 0)
    query_spot = lax.broadcasted_iota(jnp.int32, (512, 512), 1) & 255

    def fold(block, op):
        return op(block.reshape(64, 8, 512), axis=0)

    def spot_of(a, b):
        return (a * (a + 1)) // 2 + b

    def softmax_rows(o):
        a = 3 - o
        q = q_h[a].reshape(512, 128)

        def first(b, top, diagonal):
            s = mm_nt(kv_h[0, b].reshape(512, 128), q) * (scaling * math.log2(math.e))
            allowed = key_spot < length - b * 512
            if diagonal:
                allowed = allowed & (key_spot - query_spot <= 256 * y)
            s = jnp.where(allowed, s, lowest)
            scores[spot_of(a, b)] = s
            return jnp.maximum(top, fold(s, jnp.max))

        top = jnp.full((8, 512), lowest, f32)
        top = lax.fori_loop(0, a, lambda b, t: first(b, t, False), top)
        top = jnp.max(first(a, top, True), axis=0, keepdims=True)

        def second(b, total):
            e = jnp.exp2(scores[spot_of(a, b)] - top)
            scores[spot_of(a, b)] = e
            return total + fold(e, jnp.sum)

        total = lax.fori_loop(0, a + 1, second, jnp.zeros((8, 512), f32))
        shares[a] = jnp.broadcast_to(1.0 / jnp.sum(total, axis=0, keepdims=True), (8, 512))

    loop(0, 4, softmax_rows)

    tail_x.arrive()
    tails = slot_sum(tail_slots)
    line = lax.broadcasted_iota(jnp.int32, (pairs, 128), 0)
    tail = jnp.sum(jnp.where(line == 2 * d, tails[:pairs], 0.0), axis=0, keepdims=True)
    loss_out[...] = tails[pairs:] / (pairs * count)
    tail_send[...] = jnp.broadcast_to(tail, (8, 128))
    tail_core = (j // 2) % 2

    def tail_copy(b, slot, seq):
        return remote("tail", tail_send, tail_in.at[slot], b, slot, d, seq)

    for b in range(2):
        to = 4 * x + 2 * b + tail_core
        pl.when(to != j)(lambda b=b, to=to: tail_copy(b, j % 2, to).start())

        @pl.when(to == j)
        def _():
            tail_in[j % 2] = tail_send[...]

    for b in range(count):
        q_term = mm(w, four(p_cols[b]))
        d_term = mm(w_t, q_cols[b])
        for half in range(2):
            rows = pl.ds(2 * b + half, pairs, stride=chunks)
            q_terms[rows, :] = q_term[:, half * 128 : half * 128 + 128]
            d_terms[rows, :] = d_term[:, half * 128 : half * 128 + 128]
    q_slots[j] = q_terms[p_rows(j), :]
    d_slots[d] = d_terms[p_rows(d), :]
    d_term_x = Axis("d_term", "dp", lambda p: d_terms.at[p_rows(p)], lambda s: d_slots.at[s])
    q_term_x = Axis("q_term", "seq", lambda p: q_terms.at[p_rows(p)], lambda s: q_slots.at[s])
    d_term_x.send()
    q_term_x.send()

    others(lambda p: head_copy("grad", grad_stage, grad_h, p, p).wait_recv(), rank, 8)
    for b in range(2):
        source = 4 * x + 2 * c + b
        pl.when(source != j)(lambda b=b, source=source: tail_copy(0, b, source).wait_recv())
    row = lax.broadcasted_iota(jnp.int32, (512, 1), 0)
    row_token = (row & 255) + 256 * y

    def core_copy(a):
        return remote("core_sum", dkv.at[:, a, :, 1 - c], core_slots.at[a], a, a, d, over_core)

    def y_copy(a):
        return remote("y_sum", y_stage.at[a], y_slots.at[a], a, a, d, over_y)

    def x_copy(to, source):
        return remote("x_out", x_stage.at[to], x_slots.at[source], to, source, d, 4 * to + 2 * y + c)

    def dq_copy(a, e, source):
        return remote(
            "dq", dq_stage.at[a, :, e], dq_slots.at[source], 2 * a + e, source, d, 4 * a + 2 * y + e
        )

    def grad_rows(a):
        q = q_h[a].reshape(512, 128)
        spot = row_token + 512 * a
        extra = jnp.where(row < 256, tail_in[0, 0:1], tail_in[1, 0:1])
        grad = grad_h[a].reshape(512, 128).astype(f32) + jnp.where(spot == length - 1, 1.0, 0.0) * extra
        grad = jnp.where(spot < length, grad, 0.0).astype(bf16)
        share = shares[a, 0:1]

        def third(b, dots):
            low = (scores[spot_of(a, b)] * share).astype(bf16)
            prob_grad = mm_nt(kv_h[1, b].reshape(512, 128), grad)
            prob_grads[b] = prob_grad
            dkv[1, b] += mm(low, grad).reshape(2, 2, 128, 128)
            return dots + fold(low.astype(f32) * prob_grad, jnp.sum)

        dots = lax.fori_loop(0, a + 1, third, jnp.zeros((8, 512), f32))
        row_dot = jnp.sum(dots, axis=0, keepdims=True)
        factor = share * scaling
        dq_acc[...] = jnp.zeros_like(dq_acc)

        def fourth(b):
            sg = (scores[spot_of(a, b)] * factor * (prob_grads[b] - row_dot)).astype(bf16)
            dkv[0, b] += mm(sg, q).reshape(2, 2, 128, 128)
            dq_acc[...] += mm_tn(kv_h[0, b].reshape(512, 128), sg)

        loop(0, a + 1, fourth)
        dq_stage[a] = jnp.transpose(dq_acc[...]).astype(bf16).reshape(2, 2, 128, 128)

    def send_y(a):
        core_copy(a).wait_recv()
        y_stage[a] = dkv[:, a, 1 - y, c] + core_slots[a, :, 1 - y]
        y_copy(a).start()

    def send_x(a):
        y_copy(a).wait_recv()
        total = dkv[:, a, y, c] + core_slots[a, :, y] + y_slots[a]
        x_stage[a] = total.astype(bf16)

        @pl.when(a != x)
        def _():
            x_copy(a, x).start()

        @pl.when(a == x)
        def _():
            x_slots[x] = x_stage[a]

    def quarter(o):
        a = 3 - o
        grad_rows(a)
        core_copy(a).start()
        for e in range(2):

            @pl.when(2 * a + e != rank)
            def _():
                dq_copy(a, e, rank).start()

            @pl.when(2 * a + e == rank)
            def _():
                dq_slots[rank] = dq_stage[a, :, e]

        pl.when(o >= 1)(lambda: send_y(a + 1))
        pl.when(o >= 2)(lambda: send_x(a + 2))

    loop(0, 4, quarter)
    send_y(0)
    send_x(1)

    d_term_x.arrive()
    d_sum = slot_sum(d_slots)
    q_term_x.arrive()
    q_sum = slot_sum(q_slots)
    q_f32[pl.ds(0, 2 * chunks), :] = q_sum
    p_f32[...] = d_sum
    for i in range(chunks):
        part = pl.ds(i * 128, 128)
        q_grad_out[:, part] = q_f32[pl.ds(i, 2, stride=chunks), :].astype(bf16)
        d_grad_out[:, part] = p_f32[pl.ds(i, 2, stride=chunks), :].astype(bf16)
    send_x(0)

    others(lambda p: dq_copy(x, c, p).wait_recv(), rank, 8)

    def gain_fold(block):
        return jnp.sum(block.reshape(16, 8, 128), axis=0)

    def query_head(h, total):
        grad = dq_slots[h // 2, h % 2].astype(f32)
        dx, part = normed_rope_back(
            queries[:, lanes(h)].astype(f32), q_gain[...], cosine[...], sine[...], grad
        )
        q_cot[:, lanes(h)] = dx.astype(bf16)
        return total + gain_fold(part)

    q_total = lax.fori_loop(0, 16, query_head, jnp.zeros((8, 128), f32))
    others(lambda p: x_copy(p, p).wait_recv(), x, 4)

    def key_head(g, total):
        v_cot[:, lanes(g)] = x_slots[g, 1]
        dx, part = normed_rope_back(
            keys[:, lanes(g)].astype(f32), k_gain[...], cosine[...], sine[...],
            x_slots[g, 0].astype(f32),
        )
        k_cot[:, lanes(g)] = dx.astype(bf16)
        return total + gain_fold(part)

    k_total = lax.fori_loop(0, 4, key_head, jnp.zeros((8, 128), f32))
    seq_slots[j, pl.ds(0, 8)] = q_total
    seq_slots[j, pl.ds(8, 8)] = k_total
    gain_seq = Axis("gain_seq", "seq", lambda p: seq_slots.at[j], lambda s: seq_slots.at[s])
    gain_seq.send()
    gain_seq.arrive()
    dp_slots[d] = slot_sum(seq_slots)
    gain_dp = Axis("gain_dp", "dp", lambda p: dp_slots.at[d], lambda s: dp_slots.at[s])
    gain_dp.send()
    gain_dp.arrive()
    gains = slot_sum(dp_slots)
    gains_out[0:1, :] = jnp.sum(gains[:8], axis=0, keepdims=True)
    gains_out[1:2, :] = jnp.sum(gains[8:], axis=0, keepdims=True)

    for sends in (q_x, p_x, part_x, tile_x, span_x, tail_x, d_term_x, q_term_x, gain_seq, gain_dp):
        sends.sent()
    others(lambda p: kv_x(p, x).wait_send(), x, 4)
    others(lambda p: head_copy("q", q_stage, q_h, p, rank).wait_send(), rank, 8)
    others(lambda p: head_copy("grad", grad_stage, grad_h, p, rank).wait_send(), rank, 8)
    for b in range(2):
        to = 4 * x + 2 * b + tail_core
        pl.when(to != j)(lambda b=b, to=to: tail_copy(b, j % 2, to).wait_send())

    def left(a):
        kv_pass("kv_y", a, y, c, over_y).wait_send()
        kv_pass("kv_core", a, y, c, over_core).wait_send()
        kv_pass("kv_both", a, 1 - y, c, over_core).wait_send()
        core_copy(a).wait_send()
        y_copy(a).wait_send()
        pl.when(a != x)(lambda: x_copy(a, x).wait_send())
        for e in range(2):
            pl.when(2 * a + e != rank)(lambda e=e: dq_copy(a, e, rank).wait_send())

    loop(0, 4, left)


def shards(
    question_embedding_matrix,
    passage_embedding_matrix,
    positive,
    queries,
    keys,
    values,
    later_grad,
    lengths,
    q_gain,
    k_gain,
    out_weight,
):
    tokens = queries.shape[1]
    positions = lax.axis_index("seq") * tokens + jnp.arange(tokens)
    frequency = rope_base ** (-2.0 * jnp.arange(64, dtype=f32) / 128)
    angles = positions.astype(f32)[:, None] * frequency[None, :]
    cosine, sine = jnp.cos(angles), jnp.sin(angles)
    cosine = jnp.concatenate([cosine, cosine], axis=1)
    sine = jnp.concatenate([-sine, sine], axis=1)
    pos_hi = jnp.broadcast_to((positive >> 1).astype(f32)[:, None], (2, 128))
    pos_lo = jnp.broadcast_to((positive & 1).astype(f32)[:, None], (2, 128))
    out = jax.ShapeDtypeStruct
    vm = pltpu.VMEM
    sems = pltpu.SemaphoreType.DMA((len(phases), count))
    loss, query_grad, doc_grad, query_cot, key_cot, value_cot, gains = pl.pallas_call(
        whole,
        out_shape=[
            out((8, 128), f32),
            out(question_embedding_matrix.shape, bf16),
            out(passage_embedding_matrix.shape, bf16),
            out(queries.shape[1:], bf16),
            out(keys.shape[1:], bf16),
            out(values.shape[1:], bf16),
            out((2, 128), f32),
        ],
        in_specs=[pl.BlockSpec(memory_space=pltpu.SMEM)] + [VMEM] * 13,
        out_specs=[VMEM] * 7,
        scratch_shapes=[
            vm((2 * q_stride, 128), f32),
            vm((2 * q_stride, 128), bf16),
            vm((2 * chunks, 128), f32),
            vm((2 * chunks, 128), bf16),
            vm((2 * q_stride * count, 128), bf16),
            vm((2 * chunks * count, 128), bf16),
            vm((2 * q_stride * count, 128), f32),
            vm((2 * chunks * count, 128), f32),
            vm((count, pairs, 256), bf16),
            vm((count, pairs, 256), bf16),
            vm((count, pairs, 256), bf16),
            vm((count, pairs, 128), f32),
            vm((count, pairs, 128), bf16),
            vm((pairs * chunks, 128), f32),
            vm((pairs * chunks, 128), f32),
            vm((count, 2 * chunks, 128), f32),
            vm((count, 2 * chunks, 128), f32),
            vm((count, pairs + 8, 128), f32),
            vm((8, 128), f32),
            vm((2, 8, 128), f32),
            vm((4, 2, 128, 128), bf16),
            vm((8, 2, 128, 128), bf16),
            vm((8, 2, 128, 128), bf16),
            vm((2, 4, 2, 2, 128, 128), bf16),
            vm((4, 2, 2, 128, 128), bf16),
            vm((4, 2, 2, 128, 128), bf16),
            vm((10, 512, 512), f32),
            vm((4, 512, 512), f32),
            vm((4, 8, 512), f32),
            vm((128, 512), f32),
            vm((2, 4, 2, 2, 128, 128), f32),
            vm((4, 2, 2, 128, 128), bf16),
            vm((8, 2, 128, 128), bf16),
            vm((4, 2, 2, 128, 128), f32),
            vm((4, 2, 128, 128), f32),
            vm((4, 2, 128, 128), f32),
            vm((4, 2, 128, 128), bf16),
            vm((4, 2, 128, 128), bf16),
            vm((count, 16, 128), f32),
            vm((count, 16, 128), f32),
            sems,
            sems,
        ],
        compiler_params=pltpu.CompilerParams(
            collective_id=0, has_side_effects=True, vmem_limit_bytes=limit
        ),
    )(
        lengths, queries[0], keys[0], values[0], later_grad[0],
        question_embedding_matrix, passage_embedding_matrix, pos_hi, pos_lo, out_weight,
        q_gain[None, :], k_gain[None, :], cosine, sine,
    )
    return (
        loss[0, 0],
        query_grad,
        doc_grad,
        query_cot[None],
        key_cot[None],
        value_cot[None],
        gains[0],
        gains[1],
    )


def solution(mesh):
    in_specs = (
        P(("dp", "seq"), None),
        P(("dp", "seq"), None),
        P(("dp", "seq")),
        P("dp", "seq", None),
        P("dp", "seq", None),
        P("dp", "seq", None),
        P("dp", "seq", None),
        P("dp"),
        P(),
        P(),
        P("seq", "dp"),
    )
    out_specs = (
        P(),
        P(("dp", "seq"), None),
        P(("dp", "seq"), None),
        P("dp", "seq", None),
        P("dp", "seq", None),
        P("dp", "seq", None),
        P(),
        P(),
    )
    return jax.shard_map(
        shards, mesh=mesh, in_specs=in_specs, out_specs=out_specs, check_vma=False
    )
```

time: 853 us -> 117 us (0.14); the launches traced: 844 us -> 116 us
  waiting for transfers between devices: 352 us -> 0 us
  blocking collectives: 266 us -> 0 us
  Pallas kernels: 0 us -> 105 us
  other arithmetic: 75.9 us -> 1.08 us
  local copies, waits for them, and re-layouts: 61.3 us -> 9.13 us
  starting transfers between devices: 33.8 us -> 0 us
  matrix products: 29.3 us -> 0 us
  between operations: 17.7 us -> 1.33 us
    all_gather x2 -> x0, waiting for transfers between devices: 328 us -> none  [the longest x1 328 us: shards(): lax.all_gather(passage_embedding_matrix, ('dp', 'seq'), axis=0, tiled=True)]
    unnamed x1 -> x0, blocking collectives: 153 us -> none
    psum x2 -> x0, blocking collectives: 113 us -> none  [the longest x1 78.4 us: shards(): lax.psum((loss_part, q_gain_part, k_gain_part), ('dp', 'seq'))]
    pallas_call x0 -> x1, Pallas kernels: none -> 105 us  [shards(): pl.pallas_call(whole, out_shape=[out((8, 128), f32), out(question_embeddi...]
    unnamed x5 -> x0, other arithmetic: 44.9 us -> none
    all_to_all x5 -> x0, starting transfers between devices: 33.3 us -> none  [the longest x1 8.75 us: shards(): lax.all_to_all(q_send, 'seq', split_axis=2, concat_axis=1, tiled=True)]
    dot_general x22 -> x0, matrix products: 29.3 us -> none  [the longest x3 5.21 us: block_terms(): jnp.einsum('kgtd,kud->kgtu', query_rows, key_rows, preferred_element_type...]
    unnamed x90 -> x17, local copies, waits for them, and re-layouts: 32.5 us -> 6.16 us
  transfers between devices with their start and end apart: 7 -> 0, of which waited for: 4 -> 0; matrix products, arithmetic and copies ran while one was open for 12% -> 0% of each run, Pallas kernels for 0% -> 0%
where the time goes in v1:
time: 117 us; the launch traced here: 116 us
  Pallas kernels  105 us (90%)
  local copies, waits for them, and re-layouts  9.13 us (8%)
  between operations  1.33 us (1%)
    pallas_call x1, Pallas kernels, shards(): pl.pallas_call(whole, out_shape=[out((8, 128), f32), out(question_embeddi...  105 us
    unnamed x17, local copies, waits for them, and re-layouts  6.16 us

profile of v1, /device:TPU:1, one launch (start us, length us, event | category | flops | bytes accessed | tf_op | source)
XLA Modules:
  0.0 116.2 jit_solution(10766655761477668651)
XLA Ops:
  1.3 0.0 copy-start.5
  1.3 0.6 copy-done.5
  2.0 0.6 broadcast_in_dim.30.pos_lo
  2.6 0.6 broadcast_in_dim.14.pos_hi
  3.2 0.3 fusion
  3.5 0.8 pad_maximum_fusion
  4.3 104.7 %shard_map.170 = (f32[8,128]{1,0:T(8,128)}, bf16[2,4096]{1,0:T(2,128)(2,1)}, bf16[2,4096]{1,0:T(2,128)(2,1)}, bf16[128,2048]{1,0:T(8,128)(2,1)}, bf16[128,512]{1...) custom-call(s32[1]{0:T(128)S(6)} %copy.24.lengths, bf16[128,2048]{1,0:T(8,128)(2,1)} %bitcast.14, ...), custom_call_target="tpu_custom_call" | custom-call | tf_op jit(solution)/shard_map/pallas_call | solution.py:565
  109.0 0.0 copy-start.3
  109.0 1.2 %slice.9 = f32[1,1]{1,0:T(1,128)} slice(f32[8,128]{1,0:T(8,128)} %get-tuple-element.15), slice={[0:1], [0:1]} | slice | bytes 8 | tf_op jit(solution)/shard_map/slice | solution.py:631
  110.2 0.0 copy-start.4
  110.2 0.7 copy-done.4
  110.9 0.5 slice_bitcast_fusion
  111.4 0.0 copy-done.3
  111.4 0.0 copy-start.2
  111.4 0.6 copy.25
  112.0 0.1 copy-done.2
  112.1 0.6 copy.26
  112.7 0.0 copy-start.1
  112.7 1.9 %copy.27 = bf16[1,128,2048]{2,1,0:T(8,128)(2,1)} copy(bf16[1,128,2048]{2,1,0:T(8,128)(2,1)} %bitcast.16) | data formatting | bytes 1048576
  114.6 0.0 copy-done.1
  114.6 0.0 copy-start
  114.6 0.7 copy.28
  115.3 0.3 copy-done
  115.6 0.7 copy.29
  (3 shorter events, 0.0 us)
Async XLA Ops:
  1.3 0.7 copy-start.5
  109.0 2.4 %copy-start.3 = (bf16[2,4096]{1,0:T(2,128)(2,1)S(1)}, bf16[2,4096]{1,0:T(2,128)(2,1)}, u32[]{:S(2)}) copy-start(bf16[2,4096]{1,0:T(2,128)(2,1)} %get-tuple-element.40) | copy-start | bytes 49156
  110.2 0.7 copy-start.4
  111.4 0.7 copy-start.2
  112.7 1.9 %copy-start.1 = (bf16[128,512]{1,0:T(8,128)(2,1)S(1)}, bf16[128,512]{1,0:T(8,128)(2,1)}, u32[]{:S(2)}) copy-start(bf16[128,512]{1,0:T(8,128)(2,1)} %get-tuple-element.19) | copy-start | bytes 393220
  114.6 1.0 copy-start

commit v2 on v1

v2 whole, which is shorter than its diff:
```python
import functools
import math

import jax
import jax.numpy as jnp
import numpy as np
from jax import lax
from jax.experimental import pallas as pl
from jax.experimental.pallas import tpu as pltpu
from jax.sharding import PartitionSpec as P

sharpness = 0.05
epsilon = 1e-06
rope_base = 1000000.0
lowest = -1e30
MESH = pl.DeviceIdType.MESH
f32 = jnp.float32
bf16 = jnp.bfloat16
VMEM = pl.BlockSpec(memory_space=pltpu.VMEM)
limit = 58 * 1024 * 1024
count = 16
pairs = 32
chunks = 32
q_stride = 40
scaling = 128 ** (-0.5)
phases = (
    "q_y", "q_x", "q_core", "p_y", "p_z", "tile", "part", "span", "tail_part", "tail",
    "d_z", "d_y", "term_core", "term_x", "term_y", "gain_seq", "gain_dp",
    "kv_x", "kv_y", "kv_core", "kv_both", "q", "grad", "dq", "core_k", "core_v", "y_k", "y_v", "x_k", "x_v",
)
phase_of = {name: i for i, name in enumerate(phases)}


def mm(a, b):
    return lax.dot_general(a, b, (((1,), (0,)), ((), ())), preferred_element_type=f32)


def mm_nt(a, b):
    return lax.dot_general(a, b, (((1,), (1,)), ((), ())), preferred_element_type=f32)


def mm_tn(a, b):
    return lax.dot_general(a, b, (((0,), (0,)), ((), ())), preferred_element_type=f32)


def loop(first, last, step):
    def body(i, carry):
        step(i)
        return carry

    lax.fori_loop(first, last, body, 0)


def swap_halves(x):
    return pltpu.roll(x, 64, 1)


def normed_rope(x, gain, cosine, sine):
    scale = lax.rsqrt(jnp.mean(x * x, axis=-1, keepdims=True) + epsilon)
    y = x * scale * gain
    return y * cosine + swap_halves(y) * sine


def normed_rope_back(x, gain, cosine, sine, grad):
    scale = lax.rsqrt(jnp.mean(x * x, axis=-1, keepdims=True) + epsilon)
    n = x * scale
    dy = grad * cosine - swap_halves(grad) * sine
    gain_part = dy * n
    dn = dy * gain
    dx = scale * (dn - n * jnp.mean(dn * n, axis=-1, keepdims=True))
    return dx, gain_part


def slot_sum(ref):
    total = ref[0]
    for i in range(1, count):
        total = total + ref[i]
    return total


def whole(
    lengths, positive_in, table, queries, keys, values, later, q_emb, p_emb, out_w, q_gain, k_gain,
    loss_out, gains_out, q_grad_out, d_grad_out, q_cot, k_cot, v_cot,
    turn, cosine, sine,
    q_f32, p_f32, q_all, p_all, q_wide, p_wide, q_cols, p_cols, tiles,
    q_part, spans, q_terms, d_terms, core_in, q_mid, q_in, q_last, q_end,
    d_in, d_last, d_end, tail_stage, tail_slots, tail_send, tail_in,
    kv_stage, q_stage, grad_stage, kv_h, q_h, grad_h,
    grad_low, scores, prob_grads, shares, dots, dq_acc, dkv, dq_stage, dq_slots,
    core_slots, y_stage, y_slots, x_stage, x_slots, seq_slots, dp_slots,
    send_sem, recv_sem, own_sem,
):
    d, j = lax.axis_index("dp"), lax.axis_index("seq")
    x, y, c = j // 4, (j // 2) % 2, j % 2
    z, low = d // 2, d % 2
    rank = 2 * x + c
    barrier = pltpu.get_barrier_semaphore()

    def remote(name, src, dst, slot, dp, seq):
        phase = phase_of[name]
        return pltpu.make_async_remote_copy(
            src_ref=src,
            dst_ref=dst,
            send_sem=send_sem.at[phase],
            recv_sem=recv_sem.at[phase, slot],
            device_id=(dp, seq),
            device_id_type=MESH,
        )

    def bulk(name, ref):
        return remote(name, ref, ref, 0, d, j)

    def others(step, me, size=count):
        for o in range(1, size):
            step(lax.rem(me + o, size))

    others(
        lambda p: pl.semaphore_signal(barrier, inc=1, device_id=(d, p), device_id_type=MESH), j
    )
    others(
        lambda p: pl.semaphore_signal(barrier, inc=1, device_id=(p, j), device_id_type=MESH), d
    )
    turn_copy = pltpu.make_async_copy(
        table.at[pl.ds(pl.multiple_of(j * 128, 128), 128)], turn, own_sem.at[0]
    )
    turn_copy.start()

    def lanes(h):
        return pl.ds(pl.multiple_of(h * 128, 128), 128)

    def q_rows(s, size=1):
        return pl.ds(pl.multiple_of(s * 2 * q_stride, 16), size * 2 * q_stride)

    def p_rows(s, size=1):
        return pl.ds(pl.multiple_of(s * 2 * chunks, 16), size * 2 * chunks)

    place = 8 * c + 2 * x + y
    q_f32[...] = jnp.zeros_like(q_f32)
    q_own, p_own = q_emb[...].astype(f32), p_emb[...].astype(f32)
    for i in range(chunks):
        q_f32[pl.ds(i, 2, stride=q_stride), :] = q_own[:, i * 128 : i * 128 + 128]
        p_f32[pl.ds(i, 2, stride=chunks), :] = p_own[:, i * 128 : i * 128 + 128]
    for i in range(2):
        index = positive_in[i]
        spot = i * q_stride + chunks
        q_f32[spot : spot + 1, :] = jnp.full((1, 128), index >> 1, jnp.int32).astype(f32)
        q_f32[spot + 1 : spot + 2, :] = jnp.full((1, 128), index & 1, jnp.int32).astype(f32)
    q_all[q_rows(place), :] = q_f32[...].astype(bf16)
    p_all[p_rows(d), :] = p_f32[...].astype(bf16)
    turn_copy.wait()
    first_half = lax.broadcasted_iota(jnp.int32, (128, 128), 1) < 64
    turned = swap_halves(turn[...])
    cosine[...] = jnp.where(first_half, turn[...], turned)
    sine[...] = jnp.where(first_half, -turned, turn[...])

    def stage_kv(g):
        rot = normed_rope(keys[:, lanes(g)].astype(f32), k_gain[...], cosine[...], sine[...])
        kv_stage[g, 0] = rot.astype(bf16)
        kv_stage[g, 1] = values[:, lanes(g)]

    loop(0, 4, stage_kv)
    pl.semaphore_wait(barrier, 2 * (count - 1))

    over_y = 4 * x + 2 * (1 - y) + c
    over_core = 4 * x + 2 * y + (1 - c)
    over_low = d + 1 - 2 * low

    def beside(p):
        return 4 * p + 2 * y + c

    def gather(name, ref, rows, dp, seq):
        return remote(name, ref.at[rows, :], ref.at[rows, :], 0, dp, seq)

    gather("q_y", q_all, q_rows(place), d, over_y).start()
    gather("p_y", p_all, p_rows(d), over_low, j).start()

    def kv_spot(a, b, e):
        return kv_h.at[:, a, b, e]

    def kv_x(to, source):
        return remote("kv_x", kv_stage.at[to], kv_spot(source, y, c), source, d, beside(to))

    others(lambda p: kv_x(p, x).start(), x, 4)
    kv_h[:, x, y, c] = kv_stage[x]

    def kv_pass(name, a, b, e, seq):
        return remote(name, kv_spot(a, b, e), kv_spot(a, b, e), a, d, seq)

    def pass_on(a):
        kv_pass("kv_y", a, y, c, over_y).start()
        kv_pass("kv_core", a, y, c, over_core).start()

    pass_on(x)

    def stage_q(h):
        rot = normed_rope(queries[:, lanes(h)].astype(f32), q_gain[...], cosine[...], sine[...])
        q_stage[h // 2, h % 2] = rot.astype(bf16)

    def seat(r):
        return 4 * (r // 2) + 2 * y + r % 2

    def head_send(name, stage, held):
        others(
            lambda p: remote(
                name, stage.at[p], held.at[x, :, c], 0, d, seat(p)
            ).start(),
            rank,
            8,
        )
        held[x, :, c] = stage[rank]

    loop(0, 16, stage_q)
    gather("q_y", q_all, q_rows(place), d, over_y).wait_recv()
    own_pair = q_rows(8 * c + 2 * x, 2)
    others(lambda p: gather("q_x", q_all, own_pair, d, beside(p)).start(), x, 4)
    gather("p_y", p_all, p_rows(d), over_low, j).wait_recv()
    own_low = p_rows(2 * z, 2)
    others(lambda p: gather("p_z", p_all, own_low, 2 * p + low, j).start(), z, 8)
    head_send("q", q_stage, q_h)

    bulk("q_x", q_all.at[q_rows(0, 6), :]).wait_recv()
    gather("q_core", q_all, q_rows(8 * c, 8), d, over_core).start()

    def stage_grad(h):
        grad_stage[h // 2, h % 2] = later[:, lanes(h)]

    loop(0, 16, stage_grad)
    dkv[...] = jnp.zeros_like(dkv)

    bulk("p_z", p_all.at[p_rows(0, 14), :]).wait_recv()
    gather("q_core", q_all, q_rows(8 * c, 8), d, over_core).wait_recv()
    q_wide[...] = q_all[...].astype(f32)
    p_wide[...] = p_all[...].astype(f32)
    for i in range(chunks):
        half = pl.ds((i % 2) * 128, 128)
        q_cols[i // 2, :, half] = q_wide[pl.ds(i, pairs, stride=q_stride), :].astype(bf16)
        p_cols[i // 2, :, half] = p_wide[pl.ds(i, pairs, stride=chunks), :].astype(bf16)
    positive = (
        2.0 * q_wide[pl.ds(chunks, pairs, stride=q_stride), :]
        + q_wide[pl.ds(chunks + 1, pairs, stride=q_stride), :]
    )

    def four(block):
        return jnp.concatenate([block] * (128 // pairs), axis=0)

    def one(block):
        return block[:32] + block[32:64] + block[64:96] + block[96:]

    logits = mm_nt(q_cols[0], four(p_cols[0]))
    for b in range(1, count):
        logits = logits + mm_nt(q_cols[b], four(p_cols[b]))
    logits = logits / sharpness
    quarter_of = lax.broadcasted_iota(jnp.int32, (8, 128), 1) >> 5

    def pack(block):
        packed = block[:8]
        for i in range(1, 4):
            packed = jnp.where(quarter_of == i, block[8 * i : 8 * i + 8], packed)
        return packed

    tiles[j] = pack(logits)

    def tile_copy(p):
        return remote("tile", tiles.at[j], tiles.at[j], 0, d, p)

    others(lambda p: tile_copy(p).start(), j)

    def part_copy(p):
        return remote("part", q_cols.at[p], q_part.at[d], 0, p, j)

    others(lambda p: part_copy(p).start(), d)
    q_part[d] = q_cols[d]
    head_send("grad", grad_stage, grad_h)
    lane = lax.broadcasted_iota(jnp.int32, (pairs, 128), 1)
    line = lax.broadcasted_iota(jnp.int32, (pairs, 128), 0)
    real = (lane >> 5) == (line >> 3)
    base = jnp.where(real, ((lane & 31) >> 1) * pairs + (lane & 1), -(1 << 20)).astype(f32)

    def pass_arrived(a):
        kv_x(a, a).wait_recv()
        pass_on(a)

    others(pass_arrived, x, 4)

    bulk("tile", tiles.at[pl.ds(0, count - 1)]).wait_recv()
    high = tiles[0]
    for i in range(1, count):
        high = jnp.maximum(high, tiles[i])
    high = jnp.max(jnp.where(real, four(high), lowest), axis=1, keepdims=True)
    mass = jnp.zeros((pairs, 128), f32)
    hit = jnp.zeros((pairs, 128), f32)
    for i in range(count):
        tile = four(tiles[i])
        mass = mass + jnp.where(real, jnp.exp(tile - high), 0.0)
        hit = hit + jnp.where(base + 2.0 * i == positive, tile, 0.0)
    log_total = high + jnp.log(jnp.sum(mass, axis=1, keepdims=True))
    picked = jnp.sum(hit, axis=1, keepdims=True)
    loss_part = jnp.sum(log_total - picked, axis=0, keepdims=True)

    def weights_of(tile, index):
        onehot = jnp.where(base + 2.0 * index == positive, 1.0, 0.0)
        return jnp.where(real, (jnp.exp(four(tile) - log_total) - onehot) / sharpness, 0.0)

    spans[d] = pack(weights_of(tiles[0], 0.0).astype(bf16).astype(f32))

    def span_copy(p):
        return remote("span", spans.at[d], spans.at[d], 0, p, j)

    others(lambda p: span_copy(p).start(), d)
    mine = weights_of(tiles[j], j.astype(f32))
    w = mine.astype(bf16)
    w_t = one(jnp.transpose(mine)).astype(bf16)

    def pass_from_y(o):
        a = lax.rem(x + o, 4)
        kv_pass("kv_y", a, 1 - y, c, over_y).wait_recv()
        kv_pass("kv_both", a, 1 - y, c, over_core).start()

    pass_from_y(0)

    for b in range(count):
        q_term = mm(w, four(p_cols[b]))
        d_term = mm(w_t, q_cols[b])
        for half in range(2):
            rows = pl.ds(2 * b + half, pairs, stride=chunks)
            q_terms[rows, :] = q_term[:, half * 128 : half * 128 + 128]
            d_terms[rows, :] = d_term[:, half * 128 : half * 128 + 128]
    pass_from_y(1)

    bulk("part", q_part.at[pl.ds(0, count - 1)]).wait_recv()
    bulk("span", spans.at[pl.ds(0, count - 1)]).wait_recv()
    span = jnp.zeros((128, 256), f32)
    for i in range(count):
        weights = jnp.where(real, four(spans[i]), 0.0).astype(bf16)
        span = span + mm_tn(weights, q_part[i])
    span = one(span).astype(bf16)
    tail_rows = mm_nt(span, out_w[...])
    for i in range(count):
        tail_stage[i, pl.ds(0, 4)] = jnp.broadcast_to(tail_rows[2 * i : 2 * i + 1], (4, 128))
        tail_stage[i, pl.ds(4, 4)] = jnp.broadcast_to(loss_part, (4, 128))

    def tail_part(p):
        return remote("tail_part", tail_stage.at[p], tail_slots.at[d], 0, p, j)

    others(lambda p: tail_part(p).start(), d)
    tail_slots[d] = tail_stage[d]

    def d_copy(p):
        return remote("d_z", d_terms.at[p_rows(2 * p, 2), :], d_in.at[z], 0, 2 * p + low, j)

    others(lambda p: d_copy(p).start(), z, 8)
    d_in[z] = d_terms[p_rows(2 * z, 2), :]
    core_send = remote("term_core", q_terms.at[p_rows(8 * (1 - c), 8), :], core_in, 0, d, over_core)
    core_send.start()
    pass_from_y(2)
    pass_from_y(3)

    def kv_core_arrive(a):
        kv_pass("kv_core", a, y, 1 - c, over_core).wait_recv()
        kv_pass("kv_both", a, 1 - y, 1 - c, over_core).wait_recv()

    loop(0, 4, kv_core_arrive)
    bulk("q", q_stage.at[pl.ds(0, 7)]).wait_recv()
    length = lengths[0]
    key_spot = lax.broadcasted_iota(jnp.int32, (512, 512), 0)
    query_spot = lax.broadcasted_iota(jnp.int32, (512, 512), 1) & 255

    def fold(block, op):
        return op(block.reshape(64, 8, 512), axis=0)

    def spot_of(a, b):
        return (a * (a + 1)) // 2 + b

    def softmax_rows(o):
        a = 3 - o
        q = q_h[a].reshape(512, 128)

        def first(b, top, diagonal):
            s = mm_nt(kv_h[0, b].reshape(512, 128), q) * (scaling * math.log2(math.e))
            allowed = key_spot < length - b * 512
            if diagonal:
                allowed = allowed & (key_spot - query_spot <= 256 * y)
            s = jnp.where(allowed, s, lowest)
            scores[spot_of(a, b)] = s
            return jnp.maximum(top, fold(s, jnp.max))

        top = jnp.full((8, 512), lowest, f32)
        top = lax.fori_loop(0, a, lambda b, t: first(b, t, False), top)
        top = jnp.max(first(a, top, True), axis=0, keepdims=True)

        def second(b, total):
            e = jnp.exp2(scores[spot_of(a, b)] - top)
            scores[spot_of(a, b)] = e
            return total + fold(e, jnp.sum)

        total = lax.fori_loop(0, a + 1, second, jnp.zeros((8, 512), f32))
        shares[a] = jnp.broadcast_to(1.0 / jnp.sum(total, axis=0, keepdims=True), (8, 512))

    loop(0, 4, softmax_rows)

    bulk("tail_part", tail_slots.at[pl.ds(0, count - 1)]).wait_recv()
    tails = slot_sum(tail_slots)
    loss_out[...] = tails[4:5] / (pairs * count)
    tail_send[...] = jnp.broadcast_to(tails[0:1], (8, 128))

    def tail_copy(slot, seq):
        return remote("tail", tail_send, tail_in.at[slot], slot, d, seq)

    for b in range(2):
        to = 4 * x + 2 * b + y
        pl.when(to != j)(lambda to=to: tail_copy(j % 2, to).start())

        @pl.when(to == j)
        def _():
            tail_in[j % 2] = tail_send[...]

    core_send.wait_recv()
    sums = q_terms[p_rows(8 * c, 8), :] + core_in[...]
    q_mid[...] = sums.reshape(4, 128, 128)

    def term_x(p):
        return remote("term_x", q_mid.at[p], q_in.at[x], 0, d, beside(p))

    others(lambda p: term_x(p).start(), x, 4)
    q_in[x] = q_mid[x]

    bulk("grad", grad_stage.at[pl.ds(0, 7)]).wait_recv()
    for b in range(2):
        source = 4 * x + 2 * c + b
        pl.when(source != j)(lambda b=b, source=source: tail_copy(b, source).wait_recv())
    row = lax.broadcasted_iota(jnp.int32, (512, 1), 0)
    row_token = (row & 255) + 256 * y

    def core_copy(t, a):
        name = ("core_k", "core_v")[t]
        return remote(name, dkv.at[t, a, :, 1 - c], core_slots.at[t, a], a, d, over_core)

    def y_copy(t, a):
        return remote(("y_k", "y_v")[t], y_stage.at[t, a], y_slots.at[t, a], a, d, over_y)

    def x_copy(t, to):
        name = ("x_k", "x_v")[t]
        return remote(name, x_stage.at[t, to], x_slots.at[t, x], 0, d, beside(to))

    def dq_copy(a, e):
        return remote("dq", dq_stage.at[a, :, e], dq_slots.at[rank], 0, d, 4 * a + 2 * y + e)

    def send_y(t, a):
        core_copy(t, a).wait_recv()
        y_stage[t, a] = dkv[t, a, 1 - y, c] + core_slots[t, a, 1 - y]
        y_copy(t, a).start()

    def send_x(t, a):
        y_copy(t, a).wait_recv()
        total = dkv[t, a, y, c] + core_slots[t, a, y] + y_slots[t, a]
        x_stage[t, a] = total.astype(bf16)

        @pl.when(a != x)
        def _():
            x_copy(t, a).start()

        @pl.when(a == x)
        def _():
            x_slots[t, x] = x_stage[t, a]

    def make_grad(a):
        spot = row_token + 512 * a
        extra = jnp.where(row < 256, tail_in[0, 0:1], tail_in[1, 0:1])
        last = jnp.where(spot == length - 1, 1.0, 0.0)
        grad = grad_h[a].reshape(512, 128).astype(f32) + last * extra
        grad_low[a] = jnp.where(spot < length, grad, 0.0).astype(bf16)

    loop(0, 4, make_grad)
    dots[...] = jnp.zeros_like(dots)

    def value_block(o):
        b = 3 - o

        def rows(a):
            low = (scores[spot_of(a, b)] * shares[a, 0:1]).astype(bf16)
            prob_grad = mm_nt(kv_h[1, b].reshape(512, 128), grad_low[a])
            prob_grads[spot_of(a, b)] = prob_grad
            dkv[1, b] += mm(low, grad_low[a]).reshape(2, 2, 128, 128)
            dots[a] += fold(low.astype(f32) * prob_grad, jnp.sum)

        loop(b, 4, rows)
        core_copy(1, b).start()
        pl.when(o >= 1)(lambda: send_y(1, b + 1))

    loop(0, 4, value_block)

    def quarter(o):
        a = 3 - o
        q = q_h[a].reshape(512, 128)
        row_dot = jnp.sum(dots[a], axis=0, keepdims=True)
        factor = shares[a, 0:1] * scaling
        dq_acc[...] = jnp.zeros_like(dq_acc)

        def keys_of(b):
            spot = spot_of(a, b)
            sg = (scores[spot] * factor * (prob_grads[spot] - row_dot)).astype(bf16)
            dkv[0, b] += mm(sg, q).reshape(2, 2, 128, 128)
            dq_acc[...] += mm_tn(kv_h[0, b].reshape(512, 128), sg)

        loop(0, a + 1, keys_of)
        core_copy(0, a).start()
        dq_stage[a] = jnp.transpose(dq_acc[...]).astype(bf16).reshape(2, 2, 128, 128)
        for e in range(2):

            @pl.when(2 * a + e != rank)
            def _():
                dq_copy(a, e).start()

            @pl.when(2 * a + e == rank)
            def _():
                dq_slots[rank] = dq_stage[a, :, e]

        pl.when(o == 0)(lambda: send_y(1, 0))
        pl.when(o >= 1)(lambda: send_y(0, a + 1))
        send_x(1, a)
        pl.when(o >= 2)(lambda: send_x(0, a + 2))

    loop(0, 4, quarter)
    send_y(0, 0)
    bulk("term_x", q_in.at[pl.ds(0, 3)]).wait_recv()
    q_last[...] = (q_in[0] + q_in[1] + q_in[2] + q_in[3]).reshape(2, 64, 128)
    term_y = remote("term_y", q_last.at[1 - y], q_end, 0, d, over_y)
    term_y.start()
    bulk("d_z", d_in.at[pl.ds(0, 7)]).wait_recv()
    d_sum = d_in[0]
    for i in range(1, 8):
        d_sum = d_sum + d_in[i]
    d_last[...] = d_sum.reshape(2, 64, 128)
    d_y = remote("d_y", d_last.at[1 - low], d_end, 0, over_low, j)
    d_y.start()
    send_x(0, 1)

    bulk("dq", dq_slots.at[pl.ds(0, 7)]).wait_recv()

    def gain_fold(block):
        return jnp.sum(block.reshape(16, 8, 128), axis=0)

    def query_head(h, total):
        grad = dq_slots[h // 2, h % 2].astype(f32)
        dx, part = normed_rope_back(
            queries[:, lanes(h)].astype(f32), q_gain[...], cosine[...], sine[...], grad
        )
        q_cot[:, lanes(h)] = dx.astype(bf16)
        return total + gain_fold(part)

    q_total = lax.fori_loop(0, 16, query_head, jnp.zeros((8, 128), f32))
    send_x(0, 0)
    term_y.wait_recv()
    d_y.wait_recv()
    q_f32[pl.ds(0, 2 * chunks), :] = q_last[y] + q_end[...]
    p_f32[...] = d_last[low] + d_end[...]
    for i in range(chunks):
        part = pl.ds(i * 128, 128)
        q_grad_out[:, part] = q_f32[pl.ds(i, 2, stride=chunks), :].astype(bf16)
        d_grad_out[:, part] = p_f32[pl.ds(i, 2, stride=chunks), :].astype(bf16)
    bulk("x_v", x_slots.at[1, pl.ds(0, 3)]).wait_recv()
    bulk("x_k", x_slots.at[0, pl.ds(0, 3)]).wait_recv()

    def key_head(g, total):
        v_cot[:, lanes(g)] = x_slots[1, g]
        dx, part = normed_rope_back(
            keys[:, lanes(g)].astype(f32), k_gain[...], cosine[...], sine[...],
            x_slots[0, g].astype(f32),
        )
        k_cot[:, lanes(g)] = dx.astype(bf16)
        return total + gain_fold(part)

    k_total = lax.fori_loop(0, 4, key_head, jnp.zeros((8, 128), f32))
    seq_slots[j, pl.ds(0, 4)] = q_total[:4] + q_total[4:]
    seq_slots[j, pl.ds(4, 4)] = k_total[:4] + k_total[4:]

    def gain_seq(p):
        return remote("gain_seq", seq_slots.at[j], seq_slots.at[j], 0, d, p)

    others(lambda p: gain_seq(p).start(), j)
    bulk("gain_seq", seq_slots.at[pl.ds(0, count - 1)]).wait_recv()
    dp_slots[d] = slot_sum(seq_slots)

    def gain_dp(p):
        return remote("gain_dp", dp_slots.at[d], dp_slots.at[d], 0, p, j)

    others(lambda p: gain_dp(p).start(), d)
    bulk("gain_dp", dp_slots.at[pl.ds(0, count - 1)]).wait_recv()
    gains = slot_sum(dp_slots)
    gains_out[0:1, :] = jnp.sum(gains[:4], axis=0, keepdims=True)
    gains_out[1:2, :] = jnp.sum(gains[4:], axis=0, keepdims=True)

    gather("q_y", q_all, q_rows(place), d, over_y).wait_send()
    gather("p_y", p_all, p_rows(d), over_low, j).wait_send()
    gather("q_core", q_all, q_rows(8 * c, 8), d, over_core).wait_send()
    for name, ref in (
        ("q_x", q_all.at[q_rows(0, 6), :]),
        ("p_z", p_all.at[p_rows(0, 14), :]),
        ("tile", tiles.at[pl.ds(0, count - 1)]),
        ("part", q_part.at[pl.ds(0, count - 1)]),
        ("span", spans.at[pl.ds(0, count - 1)]),
        ("tail_part", tail_slots.at[pl.ds(0, count - 1)]),
        ("d_z", d_in.at[pl.ds(0, 7)]),
        ("term_x", q_in.at[pl.ds(0, 3)]),
        ("gain_seq", seq_slots.at[pl.ds(0, count - 1)]),
        ("gain_dp", dp_slots.at[pl.ds(0, count - 1)]),
        ("kv_x", kv_stage.at[pl.ds(0, 3)]),
        ("kv_y", kv_h.at[:, :, 0, 0]),
        ("kv_core", kv_h.at[:, :, 0, 0]),
        ("kv_both", kv_h.at[:, :, 0, 0]),
        ("q", q_stage.at[pl.ds(0, 7)]),
        ("grad", grad_stage.at[pl.ds(0, 7)]),
        ("dq", dq_slots.at[pl.ds(0, 7)]),
        ("core_k", core_slots.at[0]),
        ("core_v", core_slots.at[1]),
        ("y_k", y_stage.at[0]),
        ("y_v", y_stage.at[1]),
        ("x_k", x_slots.at[0, pl.ds(0, 3)]),
        ("x_v", x_slots.at[1, pl.ds(0, 3)]),
    ):
        bulk(name, ref).wait_send()
    core_send.wait_send()
    term_y.wait_send()
    d_y.wait_send()
    for b in range(2):
        to = 4 * x + 2 * b + y
        pl.when(to != j)(lambda to=to: tail_copy(j % 2, to).wait_send())


def finish(loss, gains, *refs):
    size = (len(refs) - 3) // 2
    loss_out, q_out, k_out = refs[size : size + 3]
    loss_out[...] = loss[0:1, 0:1]
    q_out[...] = gains[0:1, :]
    k_out[...] = gains[1:2, :]
    for made, out in zip(refs[:size], refs[size + 3 :]):
        out[...] = made[...]


def shards(
    question_embedding_matrix,
    passage_embedding_matrix,
    positive,
    queries,
    keys,
    values,
    later_grad,
    lengths,
    q_gain,
    k_gain,
    out_weight,
):
    angles = np.arange(2048)[:, None] * rope_base ** (-2.0 * np.arange(64) / 128)[None, :]
    table = jnp.asarray(np.concatenate([np.cos(angles), np.sin(angles)], axis=1).astype(np.float32))
    out = jax.ShapeDtypeStruct
    vm = pltpu.VMEM
    smem = pl.BlockSpec(memory_space=pltpu.SMEM)
    anywhere = pl.BlockSpec(memory_space=pl.ANY)
    results = [
        out(question_embedding_matrix.shape, bf16),
        out(passage_embedding_matrix.shape, bf16),
        out(queries.shape[1:], bf16),
        out(keys.shape[1:], bf16),
        out(values.shape[1:], bf16),
    ]
    loss, gains, *made = pl.pallas_call(
        whole,
        out_shape=[out((1, 128), f32), out((2, 128), f32)] + results,
        in_specs=[smem, smem, anywhere] + [VMEM] * 9,
        out_specs=[VMEM] * 7,
        scratch_shapes=[
            vm((128, 128), f32),
            vm((128, 128), f32),
            vm((128, 128), f32),
            vm((2 * q_stride, 128), f32),
            vm((2 * chunks, 128), f32),
            vm((2 * q_stride * count, 128), bf16),
            vm((2 * chunks * count, 128), bf16),
            vm((2 * q_stride * count, 128), f32),
            vm((2 * chunks * count, 128), f32),
            vm((count, pairs, 256), bf16),
            vm((count, pairs, 256), bf16),
            vm((count, 8, 128), f32),
            vm((count, pairs, 256), bf16),
            vm((count, 8, 128), f32),
            vm((pairs * chunks, 128), f32),
            vm((pairs * chunks, 128), f32),
            vm((pairs * chunks // 2, 128), f32),
            vm((4, 128, 128), f32),
            vm((4, 128, 128), f32),
            vm((2, 64, 128), f32),
            vm((64, 128), f32),
            vm((8, 128, 128), f32),
            vm((2, 64, 128), f32),
            vm((64, 128), f32),
            vm((count, 8, 128), f32),
            vm((count, 8, 128), f32),
            vm((8, 128), f32),
            vm((2, 8, 128), f32),
            vm((4, 2, 128, 128), bf16),
            vm((8, 2, 128, 128), bf16),
            vm((8, 2, 128, 128), bf16),
            vm((2, 4, 2, 2, 128, 128), bf16),
            vm((4, 2, 2, 128, 128), bf16),
            vm((4, 2, 2, 128, 128), bf16),
            vm((4, 512, 128), bf16),
            vm((10, 512, 512), f32),
            vm((10, 512, 512), f32),
            vm((4, 8, 512), f32),
            vm((4, 8, 512), f32),
            vm((128, 512), f32),
            vm((2, 4, 2, 2, 128, 128), f32),
            vm((4, 2, 2, 128, 128), bf16),
            vm((8, 2, 128, 128), bf16),
            vm((2, 4, 2, 128, 128), f32),
            vm((2, 4, 128, 128), f32),
            vm((2, 4, 128, 128), f32),
            vm((2, 4, 128, 128), bf16),
            vm((2, 4, 128, 128), bf16),
            vm((count, 8, 128), f32),
            vm((count, 8, 128), f32),
            pltpu.SemaphoreType.DMA((len(phases),)),
            pltpu.SemaphoreType.DMA((len(phases), 4)),
            pltpu.SemaphoreType.DMA((1,)),
        ],
        compiler_params=pltpu.CompilerParams(
            collective_id=0, has_side_effects=True, vmem_limit_bytes=limit
        ),
    )(
        lengths, positive, table, queries[0], keys[0], values[0], later_grad[0],
        question_embedding_matrix, passage_embedding_matrix, out_weight,
        q_gain[None, :], k_gain[None, :],
    )
    loss, q_gain_grad, k_gain_grad, query_grad, doc_grad, query_cot, key_cot, value_cot = (
        pl.pallas_call(
            finish,
            out_shape=[out((1, 1), f32), out((1, 128), f32), out((1, 128), f32)] + results,
            in_specs=[VMEM] * 7,
            out_specs=[VMEM] * 8,
        )(loss, gains, *made)
    )
    return (
        loss.reshape(()),
        query_grad,
        doc_grad,
        query_cot[None],
        key_cot[None],
        value_cot[None],
        q_gain_grad[0],
        k_gain_grad[0],
    )


def solution(mesh):
    in_specs = (
        P(("dp", "seq"), None),
        P(("dp", "seq"), None),
        P(("dp", "seq")),
        P("dp", "seq", None),
        P("dp", "seq", None),
        P("dp", "seq", None),
        P("dp", "seq", None),
        P("dp"),
        P(),
        P(),
        P("seq", "dp"),
    )
    out_specs = (
        P(),
        P(("dp", "seq"), None),
        P(("dp", "seq"), None),
        P("dp", "seq", None),
        P("dp", "seq", None),
        P("dp", "seq", None),
        P(),
        P(),
    )
    return jax.shard_map(
        shards, mesh=mesh, in_specs=in_specs, out_specs=out_specs, check_vma=False
    )
```

time: 117 us -> 86.2 us (0.74)
  Pallas kernels: 105 us -> 84.7 us
  local copies, waits for them, and re-layouts: 9.13 us -> 0 us
    pallas_call x1 -> x2, Pallas kernels: 105 us -> 84.7 us  [the longest x1 82.6 us: shards(): pl.pallas_call(whole, out_shape=[out((1, 128), f32), out((2, 128), f32)]...]
    unnamed x17 -> x0, local copies, waits for them, and re-layouts: 6.16 us -> none
    broadcast_in_dim x2 -> x0, local copies, waits for them, and re-layouts: 1.26 us -> none  [the longest x1 0.63 us: shards(): pos_lo = jnp.broadcast_to((positive & 1).astype(f32)[:, None], (2, 128))]
    slice x1 -> x0, local copies, waits for them, and re-layouts: 1.19 us -> none  [shards(): loss[0, 0]]
where the time goes in v2:
time: 86.2 us; the launch traced here: 86 us
  Pallas kernels  84.7 us (98%)
  between operations  1.29 us (1%)
    pallas_call x1, Pallas kernels, shards(): pl.pallas_call(whole, out_shape=[out((1, 128), f32), out((2, 128), f32)]...  82.6 us
    pallas_call x1, Pallas kernels, shards(): pl.pallas_call(finish, out_shape=[out((1, 1), f32), out((1, 128), f32), o...  2.1 us

profile of v2, /device:TPU:1, one launch (start us, length us, event | category | flops | bytes accessed | tf_op | source)
XLA Modules:
  0.0 86.0 jit_solution(10719094068491701549)
XLA Ops:
  1.3 82.6 %shard_map.179 = (f32[1,128]{1,0:T(1,128)}, f32[2,128]{1,0:T(2,128)}, bf16[2,4096]{1,0:T(2,128)(2,1)}, bf16[2,4096]{1,0:T(2,128)(2,1)}, bf16[128,2048]{1,0:T(8,1...) custom-call(s32[1]{0:T(128)S(6)} %copy.20.lengths, s32[2]{0:T(128)} %positive_in.1, ...), custom_call_target="tpu_custom_call" | custom-call | tf_op jit(solution)/shard_map/pallas_call | solution.py:666
  83.9 2.1 %shard_map.180 = (f32[1,1]{1,0:T(1,128)}, f32[1,128]{1,0:T(1,128)}, f32[1,128]{1,0:T(1,128)}, bf16[2,4096]{1,0:T(2,128)(2,1)}, bf16[2,4096]{1,0:T(2,128)(2,1)}, ...) custom-call(f32[1,128]{1,0:T(1,128)} %get-tuple-element.23.loss, ...), custom_call_target="tpu_custom_call" | custom-call | tf_op jit(solution)/shard_map/pallas_call | solution.py:735

commit v3 on v2

--- a/solution.py
+++ b/solution.py
@@ -86,7 +86,7 @@
     q_part, spans, q_terms, d_terms, core_in, q_mid, q_in, q_last, q_end,
     d_in, d_last, d_end, tail_stage, tail_slots, tail_send, tail_in,
     kv_stage, q_stage, grad_stage, kv_h, q_h, grad_h,
-    grad_low, scores, prob_grads, shares, dots, dq_acc, dkv, dq_stage, dq_slots,
+    grad_low, scores, prob_grads, shares, dots, k_turn, dq_acc, dkv, dq_stage, dq_slots,
     core_slots, y_stage, y_slots, x_stage, x_slots, seq_slots, dp_slots,
     send_sem, recv_sem, own_sem,
 ):
@@ -316,16 +316,51 @@
         kv_pass("kv_y", a, 1 - y, c, over_y).wait_recv()
         kv_pass("kv_both", a, 1 - y, c, over_core).start()
 
-    pass_from_y(0)
-
-    for b in range(count):
-        q_term = mm(w, four(p_cols[b]))
-        d_term = mm(w_t, q_cols[b])
-        for half in range(2):
-            rows = pl.ds(2 * b + half, pairs, stride=chunks)
-            q_terms[rows, :] = q_term[:, half * 128 : half * 128 + 128]
-            d_terms[rows, :] = d_term[:, half * 128 : half * 128 + 128]
-    pass_from_y(1)
+    loop(0, 4, pass_from_y)
+
+
+    def kv_core_arrive(a):
+        kv_pass("kv_core", a, y, 1 - c, over_core).wait_recv()
+        kv_pass("kv_both", a, 1 - y, 1 - c, over_core).wait_recv()
+
+    loop(0, 4, kv_core_arrive)
+    bulk("q", q_stage.at[pl.ds(0, 7)]).wait_recv()
+    length = lengths[0]
+    key_spot = lax.broadcasted_iota(jnp.int32, (512, 512), 0)
+    query_spot = lax.broadcasted_iota(jnp.int32, (512, 512), 1) & 255
+
+    def fold(block, op):
+        return op(block.reshape(64, 8, 512), axis=0)
+
+    def spot_of(a, b):
+        return (a * (a + 1)) // 2 + b
+
+    def softmax_rows(o):
+        a = 3 - o
+        q = q_h[a].reshape(512, 128)
+
+        def first(b, top, diagonal):
+            s = mm_nt(kv_h[0, b].reshape(512, 128), q) * (scaling * math.log2(math.e))
+            allowed = key_spot < length - b * 512
+            if diagonal:
+                allowed = allowed & (key_spot - query_spot <= 256 * y)
+            s = jnp.where(allowed, s, lowest)
+            scores[spot_of(a, b)] = s
+            return jnp.maximum(top, fold(s, jnp.max))
+
+        top = jnp.full((8, 512), lowest, f32)
+        top = lax.fori_loop(0, a, lambda b, t: first(b, t, False), top)
+        top = jnp.max(first(a, top, True), axis=0, keepdims=True)
+
+        def second(b, total):
+            e = jnp.exp2(scores[spot_of(a, b)] - top)
+            scores[spot_of(a, b)] = e
+            return total + fold(e, jnp.sum)
+
+        total = lax.fori_loop(0, a + 1, second, jnp.zeros((8, 512), f32))
+        shares[a] = jnp.broadcast_to(1.0 / jnp.sum(total, axis=0, keepdims=True), (8, 512))
+
+    softmax_rows(0)
 
     bulk("part", q_part.at[pl.ds(0, count - 1)]).wait_recv()
     bulk("span", spans.at[pl.ds(0, count - 1)]).wait_recv()
@@ -345,6 +380,32 @@
     others(lambda p: tail_part(p).start(), d)
     tail_slots[d] = tail_stage[d]
 
+    loop(1, 4, softmax_rows)
+
+    bulk("tail_part", tail_slots.at[pl.ds(0, count - 1)]).wait_recv()
+    tails = slot_sum(tail_slots)
+    loss_out[...] = tails[4:5] / (pairs * count)
+    tail_send[...] = jnp.broadcast_to(tails[0:1], (8, 128))
+
+    def tail_copy(slot, seq):
+        return remote("tail", tail_send, tail_in.at[slot], slot, d, seq)
+
+    for b in range(2):
+        to = 4 * x + 2 * b + y
+        pl.when(to != j)(lambda to=to: tail_copy(j % 2, to).start())
+
+        @pl.when(to == j)
+        def _():
+            tail_in[j % 2] = tail_send[...]
+
+    for b in range(count):
+        q_term = mm(w, four(p_cols[b]))
+        d_term = mm(w_t, q_cols[b])
+        for half in range(2):
+            rows = pl.ds(2 * b + half, pairs, stride=chunks)
+            q_terms[rows, :] = q_term[:, half * 128 : half * 128 + 128]
+            d_terms[rows, :] = d_term[:, half * 128 : half * 128 + 128]
+
     def d_copy(p):
         return remote("d_z", d_terms.at[p_rows(2 * p, 2), :], d_in.at[z], 0, 2 * p + low, j)
 
@@ -352,78 +413,6 @@
     d_in[z] = d_terms[p_rows(2 * z, 2), :]
     core_send = remote("term_core", q_terms.at[p_rows(8 * (1 - c), 8), :], core_in, 0, d, over_core)
     core_send.start()
-    pass_from_y(2)
-    pass_from_y(3)
-
-    def kv_core_arrive(a):
-        kv_pass("kv_core", a, y, 1 - c, over_core).wait_recv()
-        kv_pass("kv_both", a, 1 - y, 1 - c, over_core).wait_recv()
-
-    loop(0, 4, kv_core_arrive)
-    bulk("q", q_stage.at[pl.ds(0, 7)]).wait_recv()
-    length = lengths[0]
-    key_spot = lax.broadcasted_iota(jnp.int32, (512, 512), 0)
-    query_spot = lax.broadcasted_iota(jnp.int32, (512, 512), 1) & 255
-
-    def fold(block, op):
-        return op(block.reshape(64, 8, 512), axis=0)
-
-    def spot_of(a, b):
-        return (a * (a + 1)) // 2 + b
-
-    def softmax_rows(o):
-        a = 3 - o
-        q = q_h[a].reshape(512, 128)
-
-        def first(b, top, diagonal):
-            s = mm_nt(kv_h[0, b].reshape(512, 128), q) * (scaling * math.log2(math.e))
-            allowed = key_spot < length - b * 512
-            if diagonal:
-                allowed = allowed & (key_spot - query_spot <= 256 * y)
-            s = jnp.where(allowed, s, lowest)
-            scores[spot_of(a, b)] = s
-            return jnp.maximum(top, fold(s, jnp.max))
-
-        top = jnp.full((8, 512), lowest, f32)
-        top = lax.fori_loop(0, a, lambda b, t: first(b, t, False), top)
-        top = jnp.max(first(a, top, True), axis=0, keepdims=True)
-
-        def second(b, total):
-            e = jnp.exp2(scores[spot_of(a, b)] - top)
-            scores[spot_of(a, b)] = e
-            return total + fold(e, jnp.sum)
-
-        total = lax.fori_loop(0, a + 1, second, jnp.zeros((8, 512), f32))
-        shares[a] = jnp.broadcast_to(1.0 / jnp.sum(total, axis=0, keepdims=True), (8, 512))
-
-    loop(0, 4, softmax_rows)
-
-    bulk("tail_part", tail_slots.at[pl.ds(0, count - 1)]).wait_recv()
-    tails = slot_sum(tail_slots)
-    loss_out[...] = tails[4:5] / (pairs * count)
-    tail_send[...] = jnp.broadcast_to(tails[0:1], (8, 128))
-
-    def tail_copy(slot, seq):
-        return remote("tail", tail_send, tail_in.at[slot], slot, d, seq)
-
-    for b in range(2):
-        to = 4 * x + 2 * b + y
-        pl.when(to != j)(lambda to=to: tail_copy(j % 2, to).start())
-
-        @pl.when(to == j)
-        def _():
-            tail_in[j % 2] = tail_send[...]
-
-    core_send.wait_recv()
-    sums = q_terms[p_rows(8 * c, 8), :] + core_in[...]
-    q_mid[...] = sums.reshape(4, 128, 128)
-
-    def term_x(p):
-        return remote("term_x", q_mid.at[p], q_in.at[x], 0, d, beside(p))
-
-    others(lambda p: term_x(p).start(), x, 4)
-    q_in[x] = q_mid[x]
-
     bulk("grad", grad_stage.at[pl.ds(0, 7)]).wait_recv()
     for b in range(2):
         source = 4 * x + 2 * c + b
@@ -470,6 +459,10 @@
         grad = grad_h[a].reshape(512, 128).astype(f32) + last * extra
         grad_low[a] = jnp.where(spot < length, grad, 0.0).astype(bf16)
 
+    def turn_keys(b):
+        k_turn[b] = jnp.transpose(kv_h[0, b].reshape(512, 128).astype(f32)).astype(bf16)
+
+    loop(0, 4, turn_keys)
     loop(0, 4, make_grad)
     dots[...] = jnp.zeros_like(dots)
 
@@ -488,6 +481,15 @@
         pl.when(o >= 1)(lambda: send_y(1, b + 1))
 
     loop(0, 4, value_block)
+    core_send.wait_recv()
+    sums = q_terms[p_rows(8 * c, 8), :] + core_in[...]
+    q_mid[...] = sums.reshape(4, 128, 128)
+
+    def term_x(p):
+        return remote("term_x", q_mid.at[p], q_in.at[x], 0, d, beside(p))
+
+    others(lambda p: term_x(p).start(), x, 4)
+    q_in[x] = q_mid[x]
 
     def quarter(o):
         a = 3 - o
@@ -500,7 +502,7 @@
             spot = spot_of(a, b)
             sg = (scores[spot] * factor * (prob_grads[spot] - row_dot)).astype(bf16)
             dkv[0, b] += mm(sg, q).reshape(2, 2, 128, 128)
-            dq_acc[...] += mm_tn(kv_h[0, b].reshape(512, 128), sg)
+            dq_acc[...] += mm(k_turn[b], sg)
 
         loop(0, a + 1, keys_of)
         core_copy(0, a).start()
@@ -708,6 +710,7 @@
             vm((10, 512, 512), f32),
             vm((4, 8, 512), f32),
             vm((4, 8, 512), f32),
+            vm((4, 128, 512), bf16),
             vm((128, 512), f32),
             vm((2, 4, 2, 2, 128, 128), f32),
             vm((4, 2, 2, 128, 128), bf16),

time: 86.2 us -> 86.2 us (level)
  no operation moved by 1% of the time
where the time goes in v3:
time: 86.2 us; the launch traced here: 86 us
  Pallas kernels  84.7 us (98%)
  between operations  1.29 us (1%)
    pallas_call x1, Pallas kernels, shards(): pl.pallas_call(whole, out_shape=[out((1, 128), f32), out((2, 128), f32)]...  82.6 us
    pallas_call x1, Pallas kernels, shards(): pl.pallas_call(finish, out_shape=[out((1, 1), f32), out((1, 128), f32), o...  2.1 us

profile of v3, /device:TPU:1, one launch (start us, length us, event | category | flops | bytes accessed | tf_op | source)
XLA Modules:
  0.0 86.0 jit_solution(17792639466165464923)
XLA Ops:
  1.3 82.6 %shard_map.179 = (f32[1,128]{1,0:T(1,128)}, f32[2,128]{1,0:T(2,128)}, bf16[2,4096]{1,0:T(2,128)(2,1)}, bf16[2,4096]{1,0:T(2,128)(2,1)}, bf16[128,2048]{1,0:T(8,1...) custom-call(s32[1]{0:T(128)S(6)} %copy.20.lengths, s32[2]{0:T(128)} %positive_in.1, ...), custom_call_target="tpu_custom_call" | custom-call | tf_op jit(solution)/shard_map/pallas_call | solution.py:668
  83.9 2.1 %shard_map.180 = (f32[1,1]{1,0:T(1,128)}, f32[1,128]{1,0:T(1,128)}, f32[1,128]{1,0:T(1,128)}, bf16[2,4096]{1,0:T(2,128)(2,1)}, bf16[2,4096]{1,0:T(2,128)(2,1)}, ...) custom-call(f32[1,128]{1,0:T(1,128)} %get-tuple-element.23.loss, ...), custom_call_target="tpu_custom_call" | custom-call | tf_op jit(solution)/shard_map/pallas_call | solution.py:738

commit v4 on v3

--- a/solution.py
+++ b/solution.py
@@ -26,7 +26,8 @@
 phases = (
     "q_y", "q_x", "q_core", "p_y", "p_z", "tile", "part", "span", "tail_part", "tail",
     "d_z", "d_y", "term_core", "term_x", "term_y", "gain_seq", "gain_dp",
-    "kv_x", "kv_y", "kv_core", "kv_both", "q", "grad", "dq", "core_k", "core_v", "y_k", "y_v", "x_k", "x_v",
+    "k_x", "k_y", "k_core", "k_both", "v_x", "v_y", "v_core", "v_both", "q", "grad", "dq", "core_sum_k", "core_sum_v", "y_sum_k", "y_sum_v",
+    "x_out_k", "x_out_v",
 )
 phase_of = {name: i for i, name in enumerate(phases)}
 
@@ -43,12 +44,12 @@
     return lax.dot_general(a, b, (((0,), (0,)), ((), ())), preferred_element_type=f32)
 
 
-def loop(first, last, step):
+def loop(first, last, step, unroll=None):
     def body(i, carry):
         step(i)
         return carry
 
-    lax.fori_loop(first, last, body, 0)
+    lax.fori_loop(first, last, body, 0, unroll=unroll)
 
 
 def swap_halves(x):
@@ -158,7 +159,7 @@
         kv_stage[g, 0] = rot.astype(bf16)
         kv_stage[g, 1] = values[:, lanes(g)]
 
-    loop(0, 4, stage_kv)
+    loop(0, 4, stage_kv, unroll=True)
     pl.semaphore_wait(barrier, 2 * (count - 1))
 
     over_y = 4 * x + 2 * (1 - y) + c
@@ -174,23 +175,32 @@
     gather("q_y", q_all, q_rows(place), d, over_y).start()
     gather("p_y", p_all, p_rows(d), over_low, j).start()
 
-    def kv_spot(a, b, e):
-        return kv_h.at[:, a, b, e]
-
-    def kv_x(to, source):
-        return remote("kv_x", kv_stage.at[to], kv_spot(source, y, c), source, d, beside(to))
-
-    others(lambda p: kv_x(p, x).start(), x, 4)
+    def x_copies(t, step):
+        def copy(to):
+            name, src = ("k_x", "v_x")[t], kv_stage.at[to, t]
+            step(remote(name, src, kv_h.at[t, x, y, c], 0, d, beside(to)))
+
+        others(copy, x, 4)
+
+    def kv_pass(t, way, of_y, of_core, seq):
+        block = kv_h.at[t, :, of_y, of_core]
+        return remote("kv"[t] + way, block, block, 0, d, seq)
+
+    def pass_on(t):
+        bulk(("k_x", "v_x")[t], kv_h.at[t, pl.ds(0, 3), y, c]).wait_recv()
+        kv_pass(t, "_y", y, c, over_y).start()
+        kv_pass(t, "_core", y, c, over_core).start()
+
+    def pass_from_y(t):
+        kv_pass(t, "_y", 1 - y, c, over_y).wait_recv()
+        kv_pass(t, "_both", 1 - y, c, over_core).start()
+
+    def kv_arrive(t):
+        kv_pass(t, "_core", y, 1 - c, over_core).wait_recv()
+        kv_pass(t, "_both", 1 - y, 1 - c, over_core).wait_recv()
+
+    x_copies(0, lambda copy: copy.start())
     kv_h[:, x, y, c] = kv_stage[x]
-
-    def kv_pass(name, a, b, e, seq):
-        return remote(name, kv_spot(a, b, e), kv_spot(a, b, e), a, d, seq)
-
-    def pass_on(a):
-        kv_pass("kv_y", a, y, c, over_y).start()
-        kv_pass("kv_core", a, y, c, over_core).start()
-
-    pass_on(x)
 
     def stage_q(h):
         rot = normed_rope(queries[:, lanes(h)].astype(f32), q_gain[...], cosine[...], sine[...])
@@ -209,13 +219,14 @@
         )
         held[x, :, c] = stage[rank]
 
-    loop(0, 16, stage_q)
+    loop(0, 16, stage_q, unroll=4)
     gather("q_y", q_all, q_rows(place), d, over_y).wait_recv()
     own_pair = q_rows(8 * c + 2 * x, 2)
     others(lambda p: gather("q_x", q_all, own_pair, d, beside(p)).start(), x, 4)
     gather("p_y", p_all, p_rows(d), over_low, j).wait_recv()
     own_low = p_rows(2 * z, 2)
     others(lambda p: gather("p_z", p_all, own_low, 2 * p + low, j).start(), z, 8)
+    pass_on(0)
     head_send("q", q_stage, q_h)
 
     bulk("q_x", q_all.at[q_rows(0, 6), :]).wait_recv()
@@ -264,6 +275,7 @@
         return remote("tile", tiles.at[j], tiles.at[j], 0, d, p)
 
     others(lambda p: tile_copy(p).start(), j)
+    x_copies(1, lambda copy: copy.start())
 
     def part_copy(p):
         return remote("part", q_cols.at[p], q_part.at[d], 0, p, j)
@@ -276,11 +288,7 @@
     real = (lane >> 5) == (line >> 3)
     base = jnp.where(real, ((lane & 31) >> 1) * pairs + (lane & 1), -(1 << 20)).astype(f32)
 
-    def pass_arrived(a):
-        kv_x(a, a).wait_recv()
-        pass_on(a)
-
-    others(pass_arrived, x, 4)
+    pass_from_y(0)
 
     bulk("tile", tiles.at[pl.ds(0, count - 1)]).wait_recv()
     high = tiles[0]
@@ -311,19 +319,9 @@
     w = mine.astype(bf16)
     w_t = one(jnp.transpose(mine)).astype(bf16)
 
-    def pass_from_y(o):
-        a = lax.rem(x + o, 4)
-        kv_pass("kv_y", a, 1 - y, c, over_y).wait_recv()
-        kv_pass("kv_both", a, 1 - y, c, over_core).start()
-
-    loop(0, 4, pass_from_y)
-
-
-    def kv_core_arrive(a):
-        kv_pass("kv_core", a, y, 1 - c, over_core).wait_recv()
-        kv_pass("kv_both", a, 1 - y, 1 - c, over_core).wait_recv()
-
-    loop(0, 4, kv_core_arrive)
+    pass_on(1)
+
+    kv_arrive(0)
     bulk("q", q_stage.at[pl.ds(0, 7)]).wait_recv()
     length = lengths[0]
     key_spot = lax.broadcasted_iota(jnp.int32, (512, 512), 0)
@@ -380,6 +378,7 @@
     others(lambda p: tail_part(p).start(), d)
     tail_slots[d] = tail_stage[d]
 
+    pass_from_y(1)
     loop(1, 4, softmax_rows)
 
     bulk("tail_part", tail_slots.at[pl.ds(0, count - 1)]).wait_recv()
@@ -413,6 +412,7 @@
     d_in[z] = d_terms[p_rows(2 * z, 2), :]
     core_send = remote("term_core", q_terms.at[p_rows(8 * (1 - c), 8), :], core_in, 0, d, over_core)
     core_send.start()
+    kv_arrive(1)
     bulk("grad", grad_stage.at[pl.ds(0, 7)]).wait_recv()
     for b in range(2):
         source = 4 * x + 2 * c + b
@@ -421,14 +421,14 @@
     row_token = (row & 255) + 256 * y
 
     def core_copy(t, a):
-        name = ("core_k", "core_v")[t]
+        name = ("core_sum_k", "core_sum_v")[t]
         return remote(name, dkv.at[t, a, :, 1 - c], core_slots.at[t, a], a, d, over_core)
 
     def y_copy(t, a):
-        return remote(("y_k", "y_v")[t], y_stage.at[t, a], y_slots.at[t, a], a, d, over_y)
+        return remote(("y_sum_k", "y_sum_v")[t], y_stage.at[t, a], y_slots.at[t, a], a, d, over_y)
 
     def x_copy(t, to):
-        name = ("x_k", "x_v")[t]
+        name = ("x_out_k", "x_out_v")[t]
         return remote(name, x_stage.at[t, to], x_slots.at[t, x], 0, d, beside(to))
 
     def dq_copy(a, e):
@@ -550,7 +550,7 @@
         q_cot[:, lanes(h)] = dx.astype(bf16)
         return total + gain_fold(part)
 
-    q_total = lax.fori_loop(0, 16, query_head, jnp.zeros((8, 128), f32))
+    q_total = lax.fori_loop(0, 16, query_head, jnp.zeros((8, 128), f32), unroll=4)
     send_x(0, 0)
     term_y.wait_recv()
     d_y.wait_recv()
@@ -560,8 +560,8 @@
         part = pl.ds(i * 128, 128)
         q_grad_out[:, part] = q_f32[pl.ds(i, 2, stride=chunks), :].astype(bf16)
         d_grad_out[:, part] = p_f32[pl.ds(i, 2, stride=chunks), :].astype(bf16)
-    bulk("x_v", x_slots.at[1, pl.ds(0, 3)]).wait_recv()
-    bulk("x_k", x_slots.at[0, pl.ds(0, 3)]).wait_recv()
+    bulk("x_out_v", x_slots.at[1, pl.ds(0, 3)]).wait_recv()
+    bulk("x_out_k", x_slots.at[0, pl.ds(0, 3)]).wait_recv()
 
     def key_head(g, total):
         v_cot[:, lanes(g)] = x_slots[1, g]
@@ -572,7 +572,7 @@
         k_cot[:, lanes(g)] = dx.astype(bf16)
         return total + gain_fold(part)
 
-    k_total = lax.fori_loop(0, 4, key_head, jnp.zeros((8, 128), f32))
+    k_total = lax.fori_loop(0, 4, key_head, jnp.zeros((8, 128), f32), unroll=True)
     seq_slots[j, pl.ds(0, 4)] = q_total[:4] + q_total[4:]
     seq_slots[j, pl.ds(4, 4)] = k_total[:4] + k_total[4:]
 
@@ -606,19 +606,23 @@
         ("term_x", q_in.at[pl.ds(0, 3)]),
         ("gain_seq", seq_slots.at[pl.ds(0, count - 1)]),
         ("gain_dp", dp_slots.at[pl.ds(0, count - 1)]),
-        ("kv_x", kv_stage.at[pl.ds(0, 3)]),
-        ("kv_y", kv_h.at[:, :, 0, 0]),
-        ("kv_core", kv_h.at[:, :, 0, 0]),
-        ("kv_both", kv_h.at[:, :, 0, 0]),
+        ("k_x", kv_stage.at[pl.ds(0, 3), 0]),
+        ("v_x", kv_stage.at[pl.ds(0, 3), 1]),
+        ("k_y", kv_h.at[0, :, 0, 0]),
+        ("v_y", kv_h.at[1, :, 0, 0]),
+        ("k_core", kv_h.at[0, :, 0, 0]),
+        ("v_core", kv_h.at[1, :, 0, 0]),
+        ("k_both", kv_h.at[0, :, 0, 0]),
+        ("v_both", kv_h.at[1, :, 0, 0]),
         ("q", q_stage.at[pl.ds(0, 7)]),
         ("grad", grad_stage.at[pl.ds(0, 7)]),
         ("dq", dq_slots.at[pl.ds(0, 7)]),
-        ("core_k", core_slots.at[0]),
-        ("core_v", core_slots.at[1]),
-        ("y_k", y_stage.at[0]),
-        ("y_v", y_stage.at[1]),
-        ("x_k", x_slots.at[0, pl.ds(0, 3)]),
-        ("x_v", x_slots.at[1, pl.ds(0, 3)]),
+        ("core_sum_k", core_slots.at[0]),
+        ("core_sum_v", core_slots.at[1]),
+        ("y_sum_k", y_stage.at[0]),
+        ("y_sum_v", y_stage.at[1]),
+        ("x_out_k", x_slots.at[0, pl.ds(0, 3)]),
+        ("x_out_v", x_slots.at[1, pl.ds(0, 3)]),
     ):
         bulk(name, ref).wait_send()
     core_send.wait_send()

time: 86.2 us -> 83.3 us (0.966)
  Pallas kernels: 84.7 us -> 81.8 us
    pallas_call x1, Pallas kernels: 82.6 us -> 79.7 us  [shards(): pl.pallas_call(whole, out_shape=[out((1, 128), f32), out((2, 128), f32)]...]
where the time goes in v4:
time: 83.3 us; the launch traced here: 83.1 us
  Pallas kernels  81.8 us (98%)
  between operations  1.29 us (2%)
    pallas_call x1, Pallas kernels, shards(): pl.pallas_call(whole, out_shape=[out((1, 128), f32), out((2, 128), f32)]...  79.7 us
    pallas_call x1, Pallas kernels, shards(): pl.pallas_call(finish, out_shape=[out((1, 1), f32), out((1, 128), f32), o...  2.1 us

profile of v4, /device:TPU:1, one launch (start us, length us, event | category | flops | bytes accessed | tf_op | source)
XLA Modules:
  0.0 83.1 jit_solution(10749504563383396588)
XLA Ops:
  1.3 79.7 %shard_map.179 = (f32[1,128]{1,0:T(1,128)}, f32[2,128]{1,0:T(2,128)}, bf16[2,4096]{1,0:T(2,128)(2,1)}, bf16[2,4096]{1,0:T(2,128)(2,1)}, bf16[128,2048]{1,0:T(8,1...) custom-call(s32[1]{0:T(128)S(6)} %copy.20.lengths, s32[2]{0:T(128)} %positive_in.1, ...), custom_call_target="tpu_custom_call" | custom-call | tf_op jit(solution)/shard_map/pallas_call | solution.py:672
  81.0 2.1 %shard_map.180 = (f32[1,1]{1,0:T(1,128)}, f32[1,128]{1,0:T(1,128)}, f32[1,128]{1,0:T(1,128)}, bf16[2,4096]{1,0:T(2,128)(2,1)}, bf16[2,4096]{1,0:T(2,128)(2,1)}, ...) custom-call(f32[1,128]{1,0:T(1,128)} %get-tuple-element.23.loss, ...), custom_call_target="tpu_custom_call" | custom-call | tf_op jit(solution)/shard_map/pallas_call | solution.py:742

commit v5 on v4

--- a/solution.py
+++ b/solution.py
@@ -87,7 +87,7 @@
     q_part, spans, q_terms, d_terms, core_in, q_mid, q_in, q_last, q_end,
     d_in, d_last, d_end, tail_stage, tail_slots, tail_send, tail_in,
     kv_stage, q_stage, grad_stage, kv_h, q_h, grad_h,
-    grad_low, scores, prob_grads, shares, dots, k_turn, dq_acc, dkv, dq_stage, dq_slots,
+    grad_low, grad_turn, scores, tops, sums, factors, attn, k_turn, v_turn, dq_acc, dkv, dq_stage, dq_slots,
     core_slots, y_stage, y_slots, x_stage, x_slots, seq_slots, dp_slots,
     send_sem, recv_sem, own_sem,
 ):
@@ -324,39 +324,42 @@
     kv_arrive(0)
     bulk("q", q_stage.at[pl.ds(0, 7)]).wait_recv()
     length = lengths[0]
-    key_spot = lax.broadcasted_iota(jnp.int32, (512, 512), 0)
-    query_spot = lax.broadcasted_iota(jnp.int32, (512, 512), 1) & 255
-
-    def fold(block, op):
-        return op(block.reshape(64, 8, 512), axis=0)
+    key_line = lax.broadcasted_iota(jnp.int32, (128, 1), 0)
+    ahead = lax.broadcasted_iota(jnp.int32, (128, 256), 0) - lax.broadcasted_iota(
+        jnp.int32, (128, 256), 1
+    )
+    tops[...] = jnp.full_like(tops, lowest)
+    sums[...] = jnp.zeros_like(sums)
 
     def spot_of(a, b):
         return (a * (a + 1)) // 2 + b
 
     def softmax_rows(o):
         a = 3 - o
-        q = q_h[a].reshape(512, 128)
-
-        def first(b, top, diagonal):
-            s = mm_nt(kv_h[0, b].reshape(512, 128), q) * (scaling * math.log2(math.e))
-            allowed = key_spot < length - b * 512
-            if diagonal:
-                allowed = allowed & (key_spot - query_spot <= 256 * y)
-            s = jnp.where(allowed, s, lowest)
-            scores[spot_of(a, b)] = s
-            return jnp.maximum(top, fold(s, jnp.max))
-
-        top = jnp.full((8, 512), lowest, f32)
-        top = lax.fori_loop(0, a, lambda b, t: first(b, t, False), top)
-        top = jnp.max(first(a, top, True), axis=0, keepdims=True)
-
-        def second(b, total):
-            e = jnp.exp2(scores[spot_of(a, b)] - top)
-            scores[spot_of(a, b)] = e
-            return total + fold(e, jnp.sum)
-
-        total = lax.fori_loop(0, a + 1, second, jnp.zeros((8, 512), f32))
-        shares[a] = jnp.broadcast_to(1.0 / jnp.sum(total, axis=0, keepdims=True), (8, 512))
+
+        def strips(b, diagonal):
+            keys_b = kv_h[0, b].reshape(4, 128, 128)
+            for half in range(2):
+                q = q_h[a, half].reshape(256, 128)
+                across = slice(half * 256, half * 256 + 256)
+                for i in range(4):
+                    start = b * 512 + i * 128
+                    bias = jnp.where(key_line < length - start, 0.0, lowest)
+                    s = mm_nt(keys_b[i], q) * (scaling * math.log2(math.e)) + bias
+                    if diagonal:
+                        s = jnp.where(ahead <= 256 * y - i * 128, s, lowest)
+                    top = jnp.max(s, axis=0, keepdims=True)
+                    e = jnp.exp2(s - top)
+                    scores[spot_of(a, b), i * 128 : i * 128 + 128, across] = e
+                    tops[a, b, i : i + 1, across] = top
+                    sums[a, b, i : i + 1, across] = jnp.sum(e, axis=0, keepdims=True)
+
+        loop(0, a, lambda b: strips(b, False))
+        strips(a, True)
+        part_tops = tops[a].reshape(32, 512)
+        part = jnp.exp2(part_tops - jnp.max(part_tops, axis=0, keepdims=True))
+        total = jnp.sum(part * sums[a].reshape(32, 512), axis=0, keepdims=True)
+        factors[a] = (part * (1.0 / total)).reshape(4, 8, 512)
 
     softmax_rows(0)
 
@@ -459,22 +462,32 @@
         grad = grad_h[a].reshape(512, 128).astype(f32) + last * extra
         grad_low[a] = jnp.where(spot < length, grad, 0.0).astype(bf16)
 
-    def turn_keys(b):
-        k_turn[b] = jnp.transpose(kv_h[0, b].reshape(512, 128).astype(f32)).astype(bf16)
-
-    loop(0, 4, turn_keys)
+    def turned_block(block):
+        return jnp.transpose(block.reshape(512, 128).astype(f32))
+
+    def turn_block(b):
+        k_turn[b] = turned_block(kv_h[0, b]).astype(bf16)
+        v_turn[b] = turned_block(kv_h[1, b]).astype(bf16)
+        grad_turn[b] = turned_block(grad_low[b])
+
     loop(0, 4, make_grad)
-    dots[...] = jnp.zeros_like(dots)
+    loop(0, 4, turn_block)
+    attn[...] = jnp.zeros_like(attn)
 
     def value_block(o):
         b = 3 - o
 
         def rows(a):
-            low = (scores[spot_of(a, b)] * shares[a, 0:1]).astype(bf16)
-            prob_grad = mm_nt(kv_h[1, b].reshape(512, 128), grad_low[a])
-            prob_grads[spot_of(a, b)] = prob_grad
-            dkv[1, b] += mm(low, grad_low[a]).reshape(2, 2, 128, 128)
-            dots[a] += fold(low.astype(f32) * prob_grad, jnp.sum)
+            spot = spot_of(a, b)
+            low_b = jnp.concatenate(
+                [
+                    (scores[spot, i * 128 : i * 128 + 128] * factors[a, b, i : i + 1]).astype(bf16)
+                    for i in range(4)
+                ],
+                axis=0,
+            )
+            dkv[1, b] += mm(low_b, grad_low[a]).reshape(2, 2, 128, 128)
+            attn[a] += mm(v_turn[b], low_b)
 
         loop(b, 4, rows)
         core_copy(1, b).start()
@@ -482,8 +495,8 @@
 
     loop(0, 4, value_block)
     core_send.wait_recv()
-    sums = q_terms[p_rows(8 * c, 8), :] + core_in[...]
-    q_mid[...] = sums.reshape(4, 128, 128)
+    both = q_terms[p_rows(8 * c, 8), :] + core_in[...]
+    q_mid[...] = both.reshape(4, 128, 128)
 
     def term_x(p):
         return remote("term_x", q_mid.at[p], q_in.at[x], 0, d, beside(p))
@@ -494,13 +507,18 @@
     def quarter(o):
         a = 3 - o
         q = q_h[a].reshape(512, 128)
-        row_dot = jnp.sum(dots[a], axis=0, keepdims=True)
-        factor = shares[a, 0:1] * scaling
+        row_dot = jnp.sum(grad_turn[a] * attn[a], axis=0, keepdims=True)
         dq_acc[...] = jnp.zeros_like(dq_acc)
 
         def keys_of(b):
             spot = spot_of(a, b)
-            sg = (scores[spot] * factor * (prob_grads[spot] - row_dot)).astype(bf16)
+            values_b = kv_h[1, b].reshape(4, 128, 128)
+            parts = []
+            for i in range(4):
+                prob_grad = mm_nt(values_b[i], grad_low[a])
+                probs = scores[spot, i * 128 : i * 128 + 128] * (factors[a, b, i : i + 1] * scaling)
+                parts.append((probs * (prob_grad - row_dot)).astype(bf16))
+            sg = jnp.concatenate(parts, axis=0)
             dkv[0, b] += mm(sg, q).reshape(2, 2, 128, 128)
             dq_acc[...] += mm(k_turn[b], sg)
 
@@ -710,10 +728,13 @@
             vm((4, 2, 2, 128, 128), bf16),
             vm((4, 2, 2, 128, 128), bf16),
             vm((4, 512, 128), bf16),
+            vm((4, 128, 512), f32),
             vm((10, 512, 512), f32),
-            vm((10, 512, 512), f32),
-            vm((4, 8, 512), f32),
-            vm((4, 8, 512), f32),
+            vm((4, 4, 8, 512), f32),
+            vm((4, 4, 8, 512), f32),
+            vm((4, 4, 8, 512), f32),
+            vm((4, 128, 512), f32),
+            vm((4, 128, 512), bf16),
             vm((4, 128, 512), bf16),
             vm((128, 512), f32),
             vm((2, 4, 2, 2, 128, 128), f32),

time: 83.3 us -> 83.4 us (level)
  no operation moved by 1% of the time
where the time goes in v5:
time: 83.4 us; the launch traced here: 83.2 us
  Pallas kernels  81.9 us (98%)
  between operations  1.29 us (2%)
    pallas_call x1, Pallas kernels, shards(): pl.pallas_call(whole, out_shape=[out((1, 128), f32), out((2, 128), f32)]...  79.8 us
    pallas_call x1, Pallas kernels, shards(): pl.pallas_call(finish, out_shape=[out((1, 1), f32), out((1, 128), f32), o...  2.1 us

profile of v5, /device:TPU:1, one launch (start us, length us, event | category | flops | bytes accessed | tf_op | source)
XLA Modules:
  0.0 83.2 jit_solution(10268556953875391122)
XLA Ops:
  1.3 79.8 %shard_map.179 = (f32[1,128]{1,0:T(1,128)}, f32[2,128]{1,0:T(2,128)}, bf16[2,4096]{1,0:T(2,128)(2,1)}, bf16[2,4096]{1,0:T(2,128)(2,1)}, bf16[128,2048]{1,0:T(8,1...) custom-call(s32[1]{0:T(128)S(6)} %copy.20.lengths, s32[2]{0:T(128)} %positive_in.1, ...), custom_call_target="tpu_custom_call" | custom-call | tf_op jit(solution)/shard_map/pallas_call | solution.py:690
  81.1 2.1 %shard_map.180 = (f32[1,1]{1,0:T(1,128)}, f32[1,128]{1,0:T(1,128)}, f32[1,128]{1,0:T(1,128)}, bf16[2,4096]{1,0:T(2,128)(2,1)}, bf16[2,4096]{1,0:T(2,128)(2,1)}, ...) custom-call(f32[1,128]{1,0:T(1,128)} %get-tuple-element.23.loss, ...), custom_call_target="tpu_custom_call" | custom-call | tf_op jit(solution)/shard_map/pallas_call | solution.py:763

commit v6 on v5

--- a/solution.py
+++ b/solution.py
@@ -24,8 +24,8 @@
 q_stride = 40
 scaling = 128 ** (-0.5)
 phases = (
-    "q_y", "q_x", "q_core", "p_y", "p_z", "tile", "part", "span", "tail_part", "tail",
-    "d_z", "d_y", "term_core", "term_x", "term_y", "gain_seq", "gain_dp",
+    "q_y", "q_x", "q_core", "p_y", "p_z", "tile", "part", "part_core", "span", "tail_part", "tail",
+    "d_out", "term_core", "term_x", "term_y", "gain_seq", "gain_dp",
     "k_x", "k_y", "k_core", "k_both", "v_x", "v_y", "v_core", "v_both", "q", "grad", "dq", "core_sum_k", "core_sum_v", "y_sum_k", "y_sum_v",
     "x_out_k", "x_out_v",
 )
@@ -84,8 +84,8 @@
     loss_out, gains_out, q_grad_out, d_grad_out, q_cot, k_cot, v_cot,
     turn, cosine, sine,
     q_f32, p_f32, q_all, p_all, q_wide, p_wide, q_cols, p_cols, tiles,
-    q_part, spans, q_terms, d_terms, core_in, q_mid, q_in, q_last, q_end,
-    d_in, d_last, d_end, tail_stage, tail_slots, tail_send, tail_in,
+    q_part, spans, span_cat, q_terms, core_in, q_mid, q_in, q_last, q_end,
+    d_sum, d_stage, d_in, tail_stage, tail_slots, tail_send, tail_in,
     kv_stage, q_stage, grad_stage, kv_h, q_h, grad_h,
     grad_low, grad_turn, scores, tops, sums, factors, attn, k_turn, v_turn, dq_acc, dkv, dq_stage, dq_slots,
     core_slots, y_stage, y_slots, x_stage, x_slots, seq_slots, dp_slots,
@@ -277,11 +277,16 @@
     others(lambda p: tile_copy(p).start(), j)
     x_copies(1, lambda copy: copy.start())
 
+    def half_of(core):
+        return pl.ds(pl.multiple_of(16 * core, 16), 16)
+
     def part_copy(p):
-        return remote("part", q_cols.at[p], q_part.at[d], 0, p, j)
+        return remote(
+            "part", q_cols.at[p, half_of(c)], q_part.at[d, half_of(c)], 0, p, j
+        )
 
     others(lambda p: part_copy(p).start(), d)
-    q_part[d] = q_cols[d]
+    q_part[d, half_of(c)] = q_cols[d, half_of(c)]
     head_send("grad", grad_stage, grad_h)
     lane = lax.broadcasted_iota(jnp.int32, (pairs, 128), 1)
     line = lax.broadcasted_iota(jnp.int32, (pairs, 128), 0)
@@ -309,16 +314,14 @@
         onehot = jnp.where(base + 2.0 * index == positive, 1.0, 0.0)
         return jnp.where(real, (jnp.exp(four(tile) - log_total) - onehot) / sharpness, 0.0)
 
-    spans[d] = pack(weights_of(tiles[0], 0.0).astype(bf16).astype(f32))
+    mine = weights_of(tiles[j], j.astype(f32)).astype(bf16)
+    spans[d, pl.ds(0, 8)] = pack(weights_of(tiles[0], 0.0).astype(bf16).astype(f32))
+    spans[d, pl.ds(8, 8)] = pack(mine.astype(f32))
 
     def span_copy(p):
         return remote("span", spans.at[d], spans.at[d], 0, p, j)
 
     others(lambda p: span_copy(p).start(), d)
-    mine = weights_of(tiles[j], j.astype(f32))
-    w = mine.astype(bf16)
-    w_t = one(jnp.transpose(mine)).astype(bf16)
-
     pass_on(1)
 
     kv_arrive(0)
@@ -362,14 +365,28 @@
         factors[a] = (part * (1.0 / total)).reshape(4, 8, 512)
 
     softmax_rows(0)
-
-    bulk("part", q_part.at[pl.ds(0, count - 1)]).wait_recv()
+    bulk("part", q_part.at[pl.ds(0, count - 1), pl.ds(0, 16)]).wait_recv()
+    part_core = remote(
+        "part_core", q_part.at[:, half_of(c)], q_part.at[:, half_of(c)], 0, d, over_core
+    )
+    part_core.start()
+    softmax_rows(1)
+
     bulk("span", spans.at[pl.ds(0, count - 1)]).wait_recv()
-    span = jnp.zeros((128, 256), f32)
     for i in range(count):
-        weights = jnp.where(real, four(spans[i]), 0.0).astype(bf16)
-        span = span + mm_tn(weights, q_part[i])
-    span = one(span).astype(bf16)
+        for t in range(2):
+            weights = jnp.where(real, four(spans[i, t * 8 : t * 8 + 8]), 0.0)
+            span_cat[i, :, t * 128 : t * 128 + 128] = weights.astype(bf16)
+    remote(
+        "part_core", q_part.at[:, half_of(1 - c)], q_part.at[:, half_of(1 - c)], 0, d, over_core
+    ).wait_recv()
+    span_sums = mm_tn(
+        span_cat[...].reshape(pairs * count, 256), q_part[...].reshape(pairs * count, 256)
+    )
+    span = one(span_sums[:128]).astype(bf16)
+    d_sums = one(span_sums[128:])
+    d_sum[pl.ds(0, pairs), :] = d_sums[:, :128]
+    d_sum[pl.ds(pairs, pairs), :] = d_sums[:, 128:]
     tail_rows = mm_nt(span, out_w[...])
     for i in range(count):
         tail_stage[i, pl.ds(0, 4)] = jnp.broadcast_to(tail_rows[2 * i : 2 * i + 1], (4, 128))
@@ -382,7 +399,7 @@
     tail_slots[d] = tail_stage[d]
 
     pass_from_y(1)
-    loop(1, 4, softmax_rows)
+    loop(2, 4, softmax_rows)
 
     bulk("tail_part", tail_slots.at[pl.ds(0, count - 1)]).wait_recv()
     tails = slot_sum(tail_slots)
@@ -400,19 +417,27 @@
         def _():
             tail_in[j % 2] = tail_send[...]
 
+    d_stage[...] = jnp.zeros_like(d_stage)
+    for r in range(2):
+        for half in range(2):
+            d_stage[pl.ds(2 * r + half, count, stride=8), :] = d_sum[
+                pl.ds(half * pairs + r, count, stride=2), :
+            ]
+
+    def d_rows(s):
+        return pl.ds(pl.multiple_of(s * 8, 8), 8)
+
+    def d_copy(p):
+        return remote("d_out", d_stage.at[d_rows(p), :], d_in.at[d_rows(d), :], 0, p, j)
+
+    others(lambda p: d_copy(p).start(), d)
+    d_in[d_rows(d), :] = d_stage[d_rows(d), :]
+
     for b in range(count):
-        q_term = mm(w, four(p_cols[b]))
-        d_term = mm(w_t, q_cols[b])
+        q_term = mm(mine, four(p_cols[b]))
         for half in range(2):
             rows = pl.ds(2 * b + half, pairs, stride=chunks)
             q_terms[rows, :] = q_term[:, half * 128 : half * 128 + 128]
-            d_terms[rows, :] = d_term[:, half * 128 : half * 128 + 128]
-
-    def d_copy(p):
-        return remote("d_z", d_terms.at[p_rows(2 * p, 2), :], d_in.at[z], 0, 2 * p + low, j)
-
-    others(lambda p: d_copy(p).start(), z, 8)
-    d_in[z] = d_terms[p_rows(2 * z, 2), :]
     core_send = remote("term_core", q_terms.at[p_rows(8 * (1 - c), 8), :], core_in, 0, d, over_core)
     core_send.start()
     kv_arrive(1)
@@ -546,13 +571,6 @@
     q_last[...] = (q_in[0] + q_in[1] + q_in[2] + q_in[3]).reshape(2, 64, 128)
     term_y = remote("term_y", q_last.at[1 - y], q_end, 0, d, over_y)
     term_y.start()
-    bulk("d_z", d_in.at[pl.ds(0, 7)]).wait_recv()
-    d_sum = d_in[0]
-    for i in range(1, 8):
-        d_sum = d_sum + d_in[i]
-    d_last[...] = d_sum.reshape(2, 64, 128)
-    d_y = remote("d_y", d_last.at[1 - low], d_end, 0, over_low, j)
-    d_y.start()
     send_x(0, 1)
 
     bulk("dq", dq_slots.at[pl.ds(0, 7)]).wait_recv()
@@ -571,13 +589,13 @@
     q_total = lax.fori_loop(0, 16, query_head, jnp.zeros((8, 128), f32), unroll=4)
     send_x(0, 0)
     term_y.wait_recv()
-    d_y.wait_recv()
+    bulk("d_out", d_in.at[pl.ds(0, 8 * (count - 1)), :]).wait_recv()
     q_f32[pl.ds(0, 2 * chunks), :] = q_last[y] + q_end[...]
-    p_f32[...] = d_last[low] + d_end[...]
     for i in range(chunks):
         part = pl.ds(i * 128, 128)
         q_grad_out[:, part] = q_f32[pl.ds(i, 2, stride=chunks), :].astype(bf16)
-        d_grad_out[:, part] = p_f32[pl.ds(i, 2, stride=chunks), :].astype(bf16)
+        d_row = 8 * (i // 2) + i % 2
+        d_grad_out[:, part] = d_in[pl.ds(d_row, 2, stride=2), :].astype(bf16)
     bulk("x_out_v", x_slots.at[1, pl.ds(0, 3)]).wait_recv()
     bulk("x_out_k", x_slots.at[0, pl.ds(0, 3)]).wait_recv()
 
@@ -617,10 +635,10 @@
         ("q_x", q_all.at[q_rows(0, 6), :]),
         ("p_z", p_all.at[p_rows(0, 14), :]),
         ("tile", tiles.at[pl.ds(0, count - 1)]),
-        ("part", q_part.at[pl.ds(0, count - 1)]),
+        ("part", q_part.at[pl.ds(0, count - 1), pl.ds(0, 16)]),
         ("span", spans.at[pl.ds(0, count - 1)]),
         ("tail_part", tail_slots.at[pl.ds(0, count - 1)]),
-        ("d_z", d_in.at[pl.ds(0, 7)]),
+        ("d_out", d_in.at[pl.ds(0, 8 * (count - 1)), :]),
         ("term_x", q_in.at[pl.ds(0, 3)]),
         ("gain_seq", seq_slots.at[pl.ds(0, count - 1)]),
         ("gain_dp", dp_slots.at[pl.ds(0, count - 1)]),
@@ -645,7 +663,7 @@
         bulk(name, ref).wait_send()
     core_send.wait_send()
     term_y.wait_send()
-    d_y.wait_send()
+    part_core.wait_send()
     for b in range(2):
         to = 4 * x + 2 * b + y
         pl.when(to != j)(lambda to=to: tail_copy(j % 2, to).wait_send())
@@ -706,17 +724,17 @@
             vm((count, pairs, 256), bf16),
             vm((count, 8, 128), f32),
             vm((count, pairs, 256), bf16),
-            vm((count, 8, 128), f32),
-            vm((pairs * chunks, 128), f32),
+            vm((count, 16, 128), f32),
+            vm((count, pairs, 256), bf16),
             vm((pairs * chunks, 128), f32),
             vm((pairs * chunks // 2, 128), f32),
             vm((4, 128, 128), f32),
             vm((4, 128, 128), f32),
             vm((2, 64, 128), f32),
             vm((64, 128), f32),
-            vm((8, 128, 128), f32),
-            vm((2, 64, 128), f32),
-            vm((64, 128), f32),
+            vm((2 * pairs, 128), f32),
+            vm((8 * count, 128), f32),
+            vm((8 * count, 128), f32),
             vm((count, 8, 128), f32),
             vm((count, 8, 128), f32),
             vm((8, 128), f32),

time: 83.4 us -> 84.4 us (1.012)
  Pallas kernels: 81.9 us -> 83 us
    pallas_call x1, Pallas kernels: 79.8 us -> 80.9 us  [shards(): pl.pallas_call(whole, out_shape=[out((1, 128), f32), out((2, 128), f32)]...]
where the time goes in v6:
time: 84.4 us; the launch traced here: 84.2 us
  Pallas kernels  83 us (98%)
  between operations  1.29 us (2%)
    pallas_call x1, Pallas kernels, shards(): pl.pallas_call(whole, out_shape=[out((1, 128), f32), out((2, 128), f32)]...  80.9 us
    pallas_call x1, Pallas kernels, shards(): pl.pallas_call(finish, out_shape=[out((1, 1), f32), out((1, 128), f32), o...  2.1 us

profile of v6, /device:TPU:1, one launch (start us, length us, event | category | flops | bytes accessed | tf_op | source)
XLA Modules:
  0.0 84.2 jit_solution(12229530622143404992)
XLA Ops:
  1.3 80.9 %shard_map.179 = (f32[1,128]{1,0:T(1,128)}, f32[2,128]{1,0:T(2,128)}, bf16[2,4096]{1,0:T(2,128)(2,1)}, bf16[2,4096]{1,0:T(2,128)(2,1)}, bf16[128,2048]{1,0:T(8,1...) custom-call(s32[1]{0:T(128)S(6)} %copy.20.lengths, s32[2]{0:T(128)} %positive_in.1, ...), custom_call_target="tpu_custom_call" | custom-call | tf_op jit(solution)/shard_map/pallas_call | solution.py:708
  82.1 2.1 %shard_map.180 = (f32[1,1]{1,0:T(1,128)}, f32[1,128]{1,0:T(1,128)}, f32[1,128]{1,0:T(1,128)}, bf16[2,4096]{1,0:T(2,128)(2,1)}, bf16[2,4096]{1,0:T(2,128)(2,1)}, ...) custom-call(f32[1,128]{1,0:T(1,128)} %get-tuple-element.23.loss, ...), custom_call_target="tpu_custom_call" | custom-call | tf_op jit(solution)/shard_map/pallas_call | solution.py:781

commit v7 on v6

--- a/solution.py
+++ b/solution.py
@@ -24,7 +24,7 @@
 q_stride = 40
 scaling = 128 ** (-0.5)
 phases = (
-    "q_y", "q_x", "q_core", "p_y", "p_z", "tile", "part", "part_core", "span", "tail_part", "tail",
+    "q_msg", "p_msg", "tile", "part", "part_core", "span", "tail_part", "w_out",
     "d_out", "term_core", "term_x", "term_y", "gain_seq", "gain_dp",
     "k_x", "k_y", "k_core", "k_both", "v_x", "v_y", "v_core", "v_both", "q", "grad", "dq", "core_sum_k", "core_sum_v", "y_sum_k", "y_sum_v",
     "x_out_k", "x_out_v",
@@ -85,7 +85,7 @@
     turn, cosine, sine,
     q_f32, p_f32, q_all, p_all, q_wide, p_wide, q_cols, p_cols, tiles,
     q_part, spans, span_cat, q_terms, core_in, q_mid, q_in, q_last, q_end,
-    d_sum, d_stage, d_in, tail_stage, tail_slots, tail_send, tail_in,
+    d_sum, d_stage, d_in, tail_stage, tail_slots, tail_in, w_in,
     kv_stage, q_stage, grad_stage, kv_h, q_h, grad_h,
     grad_low, grad_turn, scores, tops, sums, factors, attn, k_turn, v_turn, dq_acc, dkv, dq_stage, dq_slots,
     core_slots, y_stage, y_slots, x_stage, x_slots, seq_slots, dp_slots,
@@ -169,11 +169,16 @@
     def beside(p):
         return 4 * p + 2 * y + c
 
-    def gather(name, ref, rows, dp, seq):
-        return remote(name, ref.at[rows, :], ref.at[rows, :], 0, dp, seq)
-
-    gather("q_y", q_all, q_rows(place), d, over_y).start()
-    gather("p_y", p_all, p_rows(d), over_low, j).start()
+    def q_copy(p):
+        rows = q_all.at[q_rows(place), :]
+        return remote("q_msg", rows, rows, 0, d, p)
+
+    def p_copy(p):
+        rows = p_all.at[p_rows(d), :]
+        return remote("p_msg", rows, rows, 0, p, j)
+
+    others(lambda p: q_copy(p).start(), j)
+    others(lambda p: p_copy(p).start(), d)
 
     def x_copies(t, step):
         def copy(to):
@@ -220,26 +225,32 @@
         held[x, :, c] = stage[rank]
 
     loop(0, 16, stage_q, unroll=4)
-    gather("q_y", q_all, q_rows(place), d, over_y).wait_recv()
-    own_pair = q_rows(8 * c + 2 * x, 2)
-    others(lambda p: gather("q_x", q_all, own_pair, d, beside(p)).start(), x, 4)
-    gather("p_y", p_all, p_rows(d), over_low, j).wait_recv()
-    own_low = p_rows(2 * z, 2)
-    others(lambda p: gather("p_z", p_all, own_low, 2 * p + low, j).start(), z, 8)
+
+    def w_copy(slot, seq):
+        return remote("w_out", out_w, w_in.at[slot], slot, d, seq)
+
+    def w_targets(step):
+        for b in range(2):
+            to = 4 * x + 2 * b + y
+            pl.when(to != j)(lambda to=to: step(w_copy(j % 2, to)))
+
+    w_targets(lambda copy: copy.start())
+
+    @pl.when(c == y)
+    def _():
+        w_in[j % 2] = out_w[...]
+
     pass_on(0)
     head_send("q", q_stage, q_h)
 
-    bulk("q_x", q_all.at[q_rows(0, 6), :]).wait_recv()
-    gather("q_core", q_all, q_rows(8 * c, 8), d, over_core).start()
-
     def stage_grad(h):
         grad_stage[h // 2, h % 2] = later[:, lanes(h)]
 
     loop(0, 16, stage_grad)
     dkv[...] = jnp.zeros_like(dkv)
 
-    bulk("p_z", p_all.at[p_rows(0, 14), :]).wait_recv()
-    gather("q_core", q_all, q_rows(8 * c, 8), d, over_core).wait_recv()
+    bulk("q_msg", q_all.at[q_rows(0, count - 1), :]).wait_recv()
+    bulk("p_msg", p_all.at[p_rows(0, count - 1), :]).wait_recv()
     q_wide[...] = q_all[...].astype(f32)
     p_wide[...] = p_all[...].astype(f32)
     for i in range(chunks):
@@ -387,9 +398,13 @@
     d_sums = one(span_sums[128:])
     d_sum[pl.ds(0, pairs), :] = d_sums[:, :128]
     d_sum[pl.ds(pairs, pairs), :] = d_sums[:, 128:]
-    tail_rows = mm_nt(span, out_w[...])
+    for b in range(2):
+        source = 4 * x + 2 * c + b
+        pl.when(source != j)(lambda b=b, source=source: w_copy(b, source).wait_recv())
+    rows_a, rows_b = mm_nt(span, w_in[0]), mm_nt(span, w_in[1])
     for i in range(count):
-        tail_stage[i, pl.ds(0, 4)] = jnp.broadcast_to(tail_rows[2 * i : 2 * i + 1], (4, 128))
+        tail_stage[i, pl.ds(0, 2)] = jnp.broadcast_to(rows_a[2 * i : 2 * i + 1], (2, 128))
+        tail_stage[i, pl.ds(2, 2)] = jnp.broadcast_to(rows_b[2 * i : 2 * i + 1], (2, 128))
         tail_stage[i, pl.ds(4, 4)] = jnp.broadcast_to(loss_part, (4, 128))
 
     def tail_part(p):
@@ -404,18 +419,7 @@
     bulk("tail_part", tail_slots.at[pl.ds(0, count - 1)]).wait_recv()
     tails = slot_sum(tail_slots)
     loss_out[...] = tails[4:5] / (pairs * count)
-    tail_send[...] = jnp.broadcast_to(tails[0:1], (8, 128))
-
-    def tail_copy(slot, seq):
-        return remote("tail", tail_send, tail_in.at[slot], slot, d, seq)
-
-    for b in range(2):
-        to = 4 * x + 2 * b + y
-        pl.when(to != j)(lambda to=to: tail_copy(j % 2, to).start())
-
-        @pl.when(to == j)
-        def _():
-            tail_in[j % 2] = tail_send[...]
+    tail_in[...] = tails
 
     d_stage[...] = jnp.zeros_like(d_stage)
     for r in range(2):
@@ -442,9 +446,6 @@
     core_send.start()
     kv_arrive(1)
     bulk("grad", grad_stage.at[pl.ds(0, 7)]).wait_recv()
-    for b in range(2):
-        source = 4 * x + 2 * c + b
-        pl.when(source != j)(lambda b=b, source=source: tail_copy(b, source).wait_recv())
     row = lax.broadcasted_iota(jnp.int32, (512, 1), 0)
     row_token = (row & 255) + 256 * y
 
@@ -482,7 +483,7 @@
 
     def make_grad(a):
         spot = row_token + 512 * a
-        extra = jnp.where(row < 256, tail_in[0, 0:1], tail_in[1, 0:1])
+        extra = jnp.where(row < 256, tail_in[0:1], tail_in[2:3])
         last = jnp.where(spot == length - 1, 1.0, 0.0)
         grad = grad_h[a].reshape(512, 128).astype(f32) + last * extra
         grad_low[a] = jnp.where(spot < length, grad, 0.0).astype(bf16)
@@ -628,12 +629,9 @@
     gains_out[0:1, :] = jnp.sum(gains[:4], axis=0, keepdims=True)
     gains_out[1:2, :] = jnp.sum(gains[4:], axis=0, keepdims=True)
 
-    gather("q_y", q_all, q_rows(place), d, over_y).wait_send()
-    gather("p_y", p_all, p_rows(d), over_low, j).wait_send()
-    gather("q_core", q_all, q_rows(8 * c, 8), d, over_core).wait_send()
     for name, ref in (
-        ("q_x", q_all.at[q_rows(0, 6), :]),
-        ("p_z", p_all.at[p_rows(0, 14), :]),
+        ("q_msg", q_all.at[q_rows(0, count - 1), :]),
+        ("p_msg", p_all.at[p_rows(0, count - 1), :]),
         ("tile", tiles.at[pl.ds(0, count - 1)]),
         ("part", q_part.at[pl.ds(0, count - 1), pl.ds(0, 16)]),
         ("span", spans.at[pl.ds(0, count - 1)]),
@@ -664,9 +662,7 @@
     core_send.wait_send()
     term_y.wait_send()
     part_core.wait_send()
-    for b in range(2):
-        to = 4 * x + 2 * b + y
-        pl.when(to != j)(lambda to=to: tail_copy(j % 2, to).wait_send())
+    w_targets(lambda copy: copy.wait_send())
 
 
 def finish(loss, gains, *refs):
@@ -738,7 +734,7 @@
             vm((count, 8, 128), f32),
             vm((count, 8, 128), f32),
             vm((8, 128), f32),
-            vm((2, 8, 128), f32),
+            vm((2, 128, 256), bf16),
             vm((4, 2, 128, 128), bf16),
             vm((8, 2, 128, 128), bf16),
             vm((8, 2, 128, 128), bf16),

time: 84.4 us -> 83.4 us (0.988)
  Pallas kernels: 83 us -> 81.9 us
    pallas_call x1, Pallas kernels: 80.9 us -> 79.8 us  [shards(): pl.pallas_call(whole, out_shape=[out((1, 128), f32), out((2, 128), f32)]...]
where the time goes in v7:
time: 83.4 us; the launch traced here: 83.2 us
  Pallas kernels  81.9 us (98%)
  between operations  1.29 us (2%)
    pallas_call x1, Pallas kernels, shards(): pl.pallas_call(whole, out_shape=[out((1, 128), f32), out((2, 128), f32)]...  79.8 us
    pallas_call x1, Pallas kernels, shards(): pl.pallas_call(finish, out_shape=[out((1, 1), f32), out((1, 128), f32), o...  2.1 us

profile of v7, /device:TPU:1, one launch (start us, length us, event | category | flops | bytes accessed | tf_op | source)
XLA Modules:
  0.0 83.2 jit_solution(9180416732556154318)
XLA Ops:
  1.3 79.8 %shard_map.179 = (f32[1,128]{1,0:T(1,128)}, f32[2,128]{1,0:T(2,128)}, bf16[2,4096]{1,0:T(2,128)(2,1)}, bf16[2,4096]{1,0:T(2,128)(2,1)}, bf16[128,2048]{1,0:T(8,1...) custom-call(s32[1]{0:T(128)S(6)} %copy.20.lengths, s32[2]{0:T(128)} %positive_in.1, ...), custom_call_target="tpu_custom_call" | custom-call | tf_op jit(solution)/shard_map/pallas_call | solution.py:704
  81.1 2.1 %shard_map.180 = (f32[1,1]{1,0:T(1,128)}, f32[1,128]{1,0:T(1,128)}, f32[1,128]{1,0:T(1,128)}, bf16[2,4096]{1,0:T(2,128)(2,1)}, bf16[2,4096]{1,0:T(2,128)(2,1)}, ...) custom-call(f32[1,128]{1,0:T(1,128)} %get-tuple-element.23.loss, ...), custom_call_target="tpu_custom_call" | custom-call | tf_op jit(solution)/shard_map/pallas_call | solution.py:777

commit v8 on v7

--- a/solution.py
+++ b/solution.py
@@ -87,7 +87,7 @@
     q_part, spans, span_cat, q_terms, core_in, q_mid, q_in, q_last, q_end,
     d_sum, d_stage, d_in, tail_stage, tail_slots, tail_in, w_in,
     kv_stage, q_stage, grad_stage, kv_h, q_h, grad_h,
-    grad_low, grad_turn, scores, tops, sums, factors, attn, k_turn, v_turn, dq_acc, dkv, dq_stage, dq_slots,
+    grad_low, grad_turn, grad_cat, last_probs, scores, tops, sums, factors, attn, k_turn, v_turn, dq_acc, dkv, dq_stage, dq_slots,
     core_slots, y_stage, y_slots, x_stage, x_slots, seq_slots, dp_slots,
     send_sem, recv_sem, own_sem,
 ):
@@ -112,7 +112,7 @@
         return remote(name, ref, ref, 0, d, j)
 
     def others(step, me, size=count):
-        for o in range(1, size):
+        for o in sorted(range(1, size), key=lambda o: abs(o - size // 2)):
             step(lax.rem(me + o, size))
 
     others(
@@ -416,11 +416,6 @@
     pass_from_y(1)
     loop(2, 4, softmax_rows)
 
-    bulk("tail_part", tail_slots.at[pl.ds(0, count - 1)]).wait_recv()
-    tails = slot_sum(tail_slots)
-    loss_out[...] = tails[4:5] / (pairs * count)
-    tail_in[...] = tails
-
     d_stage[...] = jnp.zeros_like(d_stage)
     for r in range(2):
         for half in range(2):
@@ -494,10 +489,20 @@
     def turn_block(b):
         k_turn[b] = turned_block(kv_h[0, b]).astype(bf16)
         v_turn[b] = turned_block(kv_h[1, b]).astype(bf16)
-        grad_turn[b] = turned_block(grad_low[b])
-
-    loop(0, 4, make_grad)
+
     loop(0, 4, turn_block)
+
+    last_lane = lax.broadcasted_iota(jnp.int32, (512, 128), 1)
+
+    def first_grad(a):
+        spot = row_token + 512 * a
+        early = jnp.where(spot < length - 1, grad_h[a].reshape(512, 128).astype(f32), 0.0)
+        grad_cat[a, :, :128] = early.astype(bf16)
+        last = jnp.where(spot == length - 1, 1.0, 0.0)
+        grad_cat[a, :, 128:] = jnp.where(last_lane == row >> 8, last, 0.0).astype(bf16)
+
+    loop(0, 4, first_grad)
+    last_probs[...] = jnp.zeros_like(last_probs)
     attn[...] = jnp.zeros_like(attn)
 
     def value_block(o):
@@ -512,12 +517,12 @@
                 ],
                 axis=0,
             )
-            dkv[1, b] += mm(low_b, grad_low[a]).reshape(2, 2, 128, 128)
+            terms = mm(low_b, grad_cat[a])
+            dkv[1, b] += terms[:, :128].reshape(2, 2, 128, 128)
+            last_probs[b] += terms[:, 128:]
             attn[a] += mm(v_turn[b], low_b)
 
         loop(b, 4, rows)
-        core_copy(1, b).start()
-        pl.when(o >= 1)(lambda: send_y(1, b + 1))
 
     loop(0, 4, value_block)
     core_send.wait_recv()
@@ -529,6 +534,32 @@
 
     others(lambda p: term_x(p).start(), x, 4)
     q_in[x] = q_mid[x]
+
+    bulk("tail_part", tail_slots.at[pl.ds(0, count - 1)]).wait_recv()
+    tails = slot_sum(tail_slots)
+    loss_out[...] = tails[4:5] / (pairs * count)
+    tail_in[...] = tails
+
+    last_grad = jnp.zeros((128, 128), f32)
+    for a in range(4):
+        last_grad = last_grad + mm_tn(grad_cat[a, :, 128:], grad_h[a].reshape(512, 128))
+    head_line = lax.broadcasted_iota(jnp.int32, (128, 128), 0)
+    both_tails = jnp.where(head_line == 0, tails[0:1], jnp.where(head_line == 1, tails[2:3], 0.0))
+    last_low = (last_grad + both_tails).astype(bf16)
+
+    def last_row(o):
+        b = 3 - o
+        dkv[1, b] += mm(last_probs[b].astype(bf16), last_low).reshape(2, 2, 128, 128)
+        core_copy(1, b).start()
+
+    loop(0, 4, last_row)
+
+    def all_grad(a):
+        make_grad(a)
+        grad_turn[a] = turned_block(grad_low[a])
+
+    loop(0, 4, all_grad)
+    loop(0, 4, lambda o: send_y(1, 3 - o))
 
     def quarter(o):
         a = 3 - o
@@ -561,7 +592,6 @@
             def _():
                 dq_slots[rank] = dq_stage[a, :, e]
 
-        pl.when(o == 0)(lambda: send_y(1, 0))
         pl.when(o >= 1)(lambda: send_y(0, a + 1))
         send_x(1, a)
         pl.when(o >= 2)(lambda: send_x(0, a + 2))
@@ -743,6 +773,8 @@
             vm((4, 2, 2, 128, 128), bf16),
             vm((4, 512, 128), bf16),
             vm((4, 128, 512), f32),
+            vm((4, 512, 256), bf16),
+            vm((4, 512, 128), f32),
             vm((10, 512, 512), f32),
             vm((4, 4, 8, 512), f32),
             vm((4, 4, 8, 512), f32),

time: 83.4 us -> 82.4 us (0.988)
  Pallas kernels: 81.9 us -> 80.9 us
    pallas_call x1, Pallas kernels: 79.8 us -> 78.8 us  [shards(): pl.pallas_call(whole, out_shape=[out((1, 128), f32), out((2, 128), f32)]...]
where the time goes in v8:
time: 82.4 us; the launch traced here: 82.2 us
  Pallas kernels  80.9 us (98%)
  between operations  1.29 us (2%)
    pallas_call x1, Pallas kernels, shards(): pl.pallas_call(whole, out_shape=[out((1, 128), f32), out((2, 128), f32)]...  78.8 us
    pallas_call x1, Pallas kernels, shards(): pl.pallas_call(finish, out_shape=[out((1, 1), f32), out((1, 128), f32), o...  2.1 us

profile of v8, /device:TPU:1, one launch (start us, length us, event | category | flops | bytes accessed | tf_op | source)
XLA Modules:
  0.0 82.2 jit_solution(13634778519545590682)
XLA Ops:
  1.3 78.8 %shard_map.179 = (f32[1,128]{1,0:T(1,128)}, f32[2,128]{1,0:T(2,128)}, bf16[2,4096]{1,0:T(2,128)(2,1)}, bf16[2,4096]{1,0:T(2,128)(2,1)}, bf16[128,2048]{1,0:T(8,1...) custom-call(s32[1]{0:T(128)S(6)} %copy.20.lengths, s32[2]{0:T(128)} %positive_in.1, ...), custom_call_target="tpu_custom_call" | custom-call | tf_op jit(solution)/shard_map/pallas_call | solution.py:734
  80.1 2.1 %shard_map.180 = (f32[1,1]{1,0:T(1,128)}, f32[1,128]{1,0:T(1,128)}, f32[1,128]{1,0:T(1,128)}, bf16[2,4096]{1,0:T(2,128)(2,1)}, bf16[2,4096]{1,0:T(2,128)(2,1)}, ...) custom-call(f32[1,128]{1,0:T(1,128)} %get-tuple-element.23.loss, ...), custom_call_target="tpu_custom_call" | custom-call | tf_op jit(solution)/shard_map/pallas_call | solution.py:809

commit v9 on v8

--- a/solution.py
+++ b/solution.py
@@ -27,7 +27,7 @@
     "q_msg", "p_msg", "tile", "part", "part_core", "span", "tail_part", "w_out",
     "d_out", "term_core", "term_x", "term_y", "gain_seq", "gain_dp",
     "k_x", "k_y", "k_core", "k_both", "v_x", "v_y", "v_core", "v_both", "q", "grad", "dq", "core_sum_k", "core_sum_v", "y_sum_k", "y_sum_v",
-    "x_out_k", "x_out_v",
+    "x_out_k", "x_out_v", "last",
 )
 phase_of = {name: i for i, name in enumerate(phases)}
 
@@ -87,7 +87,7 @@
     q_part, spans, span_cat, q_terms, core_in, q_mid, q_in, q_last, q_end,
     d_sum, d_stage, d_in, tail_stage, tail_slots, tail_in, w_in,
     kv_stage, q_stage, grad_stage, kv_h, q_h, grad_h,
-    grad_low, grad_turn, grad_cat, last_probs, scores, tops, sums, factors, attn, k_turn, v_turn, dq_acc, dkv, dq_stage, dq_slots,
+    grad_low, grad_turn, grad_cat, stats, last_send, last_in, last_rows, scores, tops, sums, factors, attn, k_turn, v_turn, dq_acc, dkv, dq_stage, dq_slots,
     core_slots, y_stage, y_slots, x_stage, x_slots, seq_slots, dp_slots,
     send_sem, recv_sem, own_sem,
 ):
@@ -371,9 +371,12 @@
         loop(0, a, lambda b: strips(b, False))
         strips(a, True)
         part_tops = tops[a].reshape(32, 512)
-        part = jnp.exp2(part_tops - jnp.max(part_tops, axis=0, keepdims=True))
+        peak = jnp.max(part_tops, axis=0, keepdims=True)
+        part = jnp.exp2(part_tops - peak)
         total = jnp.sum(part * sums[a].reshape(32, 512), axis=0, keepdims=True)
         factors[a] = (part * (1.0 / total)).reshape(4, 8, 512)
+        stats[a, 0:1] = peak
+        stats[a, 1:2] = 1.0 / total
 
     softmax_rows(0)
     bulk("part", q_part.at[pl.ds(0, count - 1), pl.ds(0, 16)]).wait_recv()
@@ -466,6 +469,8 @@
     def send_x(t, a):
         y_copy(t, a).wait_recv()
         total = dkv[t, a, y, c] + core_slots[t, a, y] + y_slots[t, a]
+        if t == 1:
+            total = total + last_term(a)
         x_stage[t, a] = total.astype(bf16)
 
         @pl.when(a != x)
@@ -502,7 +507,6 @@
         grad_cat[a, :, 128:] = jnp.where(last_lane == row >> 8, last, 0.0).astype(bf16)
 
     loop(0, 4, first_grad)
-    last_probs[...] = jnp.zeros_like(last_probs)
     attn[...] = jnp.zeros_like(attn)
 
     def value_block(o):
@@ -517,12 +521,12 @@
                 ],
                 axis=0,
             )
-            terms = mm(low_b, grad_cat[a])
-            dkv[1, b] += terms[:, :128].reshape(2, 2, 128, 128)
-            last_probs[b] += terms[:, 128:]
+            dkv[1, b] += mm(low_b, grad_cat[a, :, :128]).reshape(2, 2, 128, 128)
             attn[a] += mm(v_turn[b], low_b)
 
         loop(b, 4, rows)
+        core_copy(1, b).start()
+        pl.when(o >= 1)(lambda: send_y(1, b + 1))
 
     loop(0, 4, value_block)
     core_send.wait_recv()
@@ -535,31 +539,58 @@
     others(lambda p: term_x(p).start(), x, 4)
     q_in[x] = q_mid[x]
 
+    send_y(1, 0)
+
     bulk("tail_part", tail_slots.at[pl.ds(0, count - 1)]).wait_recv()
     tails = slot_sum(tail_slots)
     loss_out[...] = tails[4:5] / (pairs * count)
     tail_in[...] = tails
 
-    last_grad = jnp.zeros((128, 128), f32)
+    last_query, last_grad = jnp.zeros((128, 128), f32), jnp.zeros((128, 128), f32)
+    row_lane = lax.broadcasted_iota(jnp.int32, (1, 512), 1)
+    peaks, parts_of = [0.0, 0.0], [0.0, 0.0]
     for a in range(4):
+        last_query = last_query + mm_tn(grad_cat[a, :, 128:], q_h[a].reshape(512, 128))
         last_grad = last_grad + mm_tn(grad_cat[a, :, 128:], grad_h[a].reshape(512, 128))
-    head_line = lax.broadcasted_iota(jnp.int32, (128, 128), 0)
-    both_tails = jnp.where(head_line == 0, tails[0:1], jnp.where(head_line == 1, tails[2:3], 0.0))
-    last_low = (last_grad + both_tails).astype(bf16)
-
-    def last_row(o):
-        b = 3 - o
-        dkv[1, b] += mm(last_probs[b].astype(bf16), last_low).reshape(2, 2, 128, 128)
-        core_copy(1, b).start()
-
-    loop(0, 4, last_row)
+        found = (row_lane & 255) + 256 * y + 512 * a == length - 1
+        for h in range(2):
+            mine_too = found & (row_lane >> 8 == h)
+            for held, line_of in ((peaks, 0), (parts_of, 1)):
+                value = jnp.where(mine_too, stats[a, line_of : line_of + 1], 0.0)
+                held[h] = held[h] + jnp.sum(value, axis=1, keepdims=True)
+    last_send[0:2] = last_query[0:2]
+    for h in range(2):
+        low = (last_grad[h : h + 1] + tails[2 * h : 2 * h + 1]).astype(bf16)
+        last_send[2 + h : 3 + h] = low.astype(f32)
+        last_send[4 + h : 5 + h] = jnp.broadcast_to(peaks[h], (1, 128))
+        last_send[6 + h : 7 + h] = jnp.broadcast_to(parts_of[h], (1, 128))
+    here = 2 * y + c
+
+    def last_copy(p):
+        return remote("last", last_send, last_in.at[here], 0, d, 4 * x + p)
+
+    others(lambda p: last_copy(p).start(), here, 4)
+    last_in[here] = last_send[...]
+
+    def last_arrive():
+        bulk("last", last_in.at[pl.ds(0, 3)]).wait_recv()
+        for p in range(4):
+            for kind in range(4):
+                last_rows[kind, 2 * p : 2 * p + 2] = last_in[p, 2 * kind : 2 * kind + 2]
+
+    def last_term(a):
+        keys_a = kv_h[0, a, y, c]
+        s = mm_nt(last_rows[0].astype(bf16), keys_a) * (scaling * math.log2(math.e))
+        key = 512 * a + 256 * y + 128 * c + lax.broadcasted_iota(jnp.int32, (8, 128), 1)
+        s = jnp.where(key < length, s, lowest)
+        low = (jnp.exp2(s - last_rows[2]) * last_rows[3]).astype(bf16)
+        return mm_tn(low, last_rows[1].astype(bf16))
 
     def all_grad(a):
         make_grad(a)
         grad_turn[a] = turned_block(grad_low[a])
 
     loop(0, 4, all_grad)
-    loop(0, 4, lambda o: send_y(1, 3 - o))
 
     def quarter(o):
         a = 3 - o
@@ -593,6 +624,7 @@
                 dq_slots[rank] = dq_stage[a, :, e]
 
         pl.when(o >= 1)(lambda: send_y(0, a + 1))
+        pl.when(o == 0)(last_arrive)
         send_x(1, a)
         pl.when(o >= 2)(lambda: send_x(0, a + 2))
 
@@ -687,6 +719,7 @@
         ("y_sum_v", y_stage.at[1]),
         ("x_out_k", x_slots.at[0, pl.ds(0, 3)]),
         ("x_out_v", x_slots.at[1, pl.ds(0, 3)]),
+        ("last", last_in.at[pl.ds(0, 3)]),
     ):
         bulk(name, ref).wait_send()
     core_send.wait_send()
@@ -774,7 +807,10 @@
             vm((4, 512, 128), bf16),
             vm((4, 128, 512), f32),
             vm((4, 512, 256), bf16),
-            vm((4, 512, 128), f32),
+            vm((4, 8, 512), f32),
+            vm((8, 128), f32),
+            vm((4, 8, 128), f32),
+            vm((4, 8, 128), f32),
             vm((10, 512, 512), f32),
             vm((4, 4, 8, 512), f32),
             vm((4, 4, 8, 512), f32),

time: 82.4 us -> 82.5 us (level)
  no operation moved by 1% of the time
where the time goes in v9:
time: 82.5 us; the launch traced here: 82.3 us
  Pallas kernels  81 us (98%)
  between operations  1.29 us (2%)
    pallas_call x1, Pallas kernels, shards(): pl.pallas_call(whole, out_shape=[out((1, 128), f32), out((2, 128), f32)]...  78.9 us
    pallas_call x1, Pallas kernels, shards(): pl.pallas_call(finish, out_shape=[out((1, 1), f32), out((1, 128), f32), o...  2.1 us

profile of v9, /device:TPU:1, one launch (start us, length us, event | category | flops | bytes accessed | tf_op | source)
XLA Modules:
  0.0 82.3 jit_solution(7184362905942036452)
XLA Ops:
  1.3 78.9 %shard_map.179 = (f32[1,128]{1,0:T(1,128)}, f32[2,128]{1,0:T(2,128)}, bf16[2,4096]{1,0:T(2,128)(2,1)}, bf16[2,4096]{1,0:T(2,128)(2,1)}, bf16[128,2048]{1,0:T(8,1...) custom-call(s32[1]{0:T(128)S(6)} %copy.20.lengths, s32[2]{0:T(128)} %positive_in.1, ...), custom_call_target="tpu_custom_call" | custom-call | tf_op jit(solution)/shard_map/pallas_call | solution.py:767
  80.2 2.1 %shard_map.180 = (f32[1,1]{1,0:T(1,128)}, f32[1,128]{1,0:T(1,128)}, f32[1,128]{1,0:T(1,128)}, bf16[2,4096]{1,0:T(2,128)(2,1)}, bf16[2,4096]{1,0:T(2,128)(2,1)}, ...) custom-call(f32[1,128]{1,0:T(1,128)} %get-tuple-element.23.loss, ...), custom_call_target="tpu_custom_call" | custom-call | tf_op jit(solution)/shard_map/pallas_call | solution.py:845

commit v10 on v8

--- a/solution.py
+++ b/solution.py
@@ -246,7 +246,7 @@
     def stage_grad(h):
         grad_stage[h // 2, h % 2] = later[:, lanes(h)]
 
-    loop(0, 16, stage_grad)
+    loop(0, 16, stage_grad, unroll=4)
     dkv[...] = jnp.zeros_like(dkv)
 
     bulk("q_msg", q_all.at[q_rows(0, count - 1), :]).wait_recv()
@@ -286,8 +286,6 @@
         return remote("tile", tiles.at[j], tiles.at[j], 0, d, p)
 
     others(lambda p: tile_copy(p).start(), j)
-    x_copies(1, lambda copy: copy.start())
-
     def half_of(core):
         return pl.ds(pl.multiple_of(16 * core, 16), 16)
 
@@ -298,7 +296,6 @@
 
     others(lambda p: part_copy(p).start(), d)
     q_part[d, half_of(c)] = q_cols[d, half_of(c)]
-    head_send("grad", grad_stage, grad_h)
     lane = lax.broadcasted_iota(jnp.int32, (pairs, 128), 1)
     line = lax.broadcasted_iota(jnp.int32, (pairs, 128), 0)
     real = (lane >> 5) == (line >> 3)
@@ -333,8 +330,8 @@
         return remote("span", spans.at[d], spans.at[d], 0, p, j)
 
     others(lambda p: span_copy(p).start(), d)
-    pass_on(1)
-
+    x_copies(1, lambda copy: copy.start())
+    head_send("grad", grad_stage, grad_h)
     kv_arrive(0)
     bulk("q", q_stage.at[pl.ds(0, 7)]).wait_recv()
     length = lengths[0]
@@ -381,6 +378,7 @@
         "part_core", q_part.at[:, half_of(c)], q_part.at[:, half_of(c)], 0, d, over_core
     )
     part_core.start()
+    pass_on(1)
     softmax_rows(1)
 
     bulk("span", spans.at[pl.ds(0, count - 1)]).wait_recv()

time: 82.4 us -> 84.5 us (1.025)
  Pallas kernels: 80.9 us -> 83.1 us
    pallas_call x1, Pallas kernels: 78.8 us -> 81 us  [shards(): pl.pallas_call(whole, out_shape=[out((1, 128), f32), out((2, 128), f32)]...]
where the time goes in v10:
time: 84.5 us; the launch traced here: 84.4 us
  Pallas kernels  83.1 us (98%)
  between operations  1.29 us (2%)
    pallas_call x1, Pallas kernels, shards(): pl.pallas_call(whole, out_shape=[out((1, 128), f32), out((2, 128), f32)]...  81 us
    pallas_call x1, Pallas kernels, shards(): pl.pallas_call(finish, out_shape=[out((1, 1), f32), out((1, 128), f32), o...  2.1 us

profile of v10, /device:TPU:1, one launch (start us, length us, event | category | flops | bytes accessed | tf_op | source)
XLA Modules:
  0.0 84.4 jit_solution(6244224617920324216)
XLA Ops:
  1.3 81.0 %shard_map.179 = (f32[1,128]{1,0:T(1,128)}, f32[2,128]{1,0:T(2,128)}, bf16[2,4096]{1,0:T(2,128)(2,1)}, bf16[2,4096]{1,0:T(2,128)(2,1)}, bf16[128,2048]{1,0:T(8,1...) custom-call(s32[1]{0:T(128)S(6)} %copy.20.lengths, s32[2]{0:T(128)} %positive_in.1, ...), custom_call_target="tpu_custom_call" | custom-call | tf_op jit(solution)/shard_map/pallas_call | solution.py:732
  82.3 2.1 %shard_map.180 = (f32[1,1]{1,0:T(1,128)}, f32[1,128]{1,0:T(1,128)}, f32[1,128]{1,0:T(1,128)}, bf16[2,4096]{1,0:T(2,128)(2,1)}, bf16[2,4096]{1,0:T(2,128)(2,1)}, ...) custom-call(f32[1,128]{1,0:T(1,128)} %get-tuple-element.23.loss, ...), custom_call_target="tpu_custom_call" | custom-call | tf_op jit(solution)/shard_map/pallas_call | solution.py:807

commit v11 on v8

--- a/solution.py
+++ b/solution.py
@@ -604,6 +604,7 @@
     term_y.start()
     send_x(0, 1)
 
+    send_x(0, 0)
     bulk("dq", dq_slots.at[pl.ds(0, 7)]).wait_recv()
 
     def gain_fold(block):
@@ -617,8 +618,7 @@
         q_cot[:, lanes(h)] = dx.astype(bf16)
         return total + gain_fold(part)
 
-    q_total = lax.fori_loop(0, 16, query_head, jnp.zeros((8, 128), f32), unroll=4)
-    send_x(0, 0)
+    q_total = lax.fori_loop(0, 16, query_head, jnp.zeros((8, 128), f32), unroll=8)
     term_y.wait_recv()
     bulk("d_out", d_in.at[pl.ds(0, 8 * (count - 1)), :]).wait_recv()
     q_f32[pl.ds(0, 2 * chunks), :] = q_last[y] + q_end[...]

time: 82.4 us -> 81.9 us (level)
  no operation moved by 1% of the time
where the time goes in v11:
time: 81.9 us; the launch traced here: 81.6 us
  Pallas kernels  80.4 us (98%)
  between operations  1.29 us (2%)
    pallas_call x1, Pallas kernels, shards(): pl.pallas_call(whole, out_shape=[out((1, 128), f32), out((2, 128), f32)]...  78.3 us
    pallas_call x1, Pallas kernels, shards(): pl.pallas_call(finish, out_shape=[out((1, 1), f32), out((1, 128), f32), o...  2.1 us

profile of v11, /device:TPU:1, one launch (start us, length us, event | category | flops | bytes accessed | tf_op | source)
XLA Modules:
  0.0 81.6 jit_solution(2463930284603169568)
XLA Ops:
  1.3 78.3 %shard_map.179 = (f32[1,128]{1,0:T(1,128)}, f32[2,128]{1,0:T(2,128)}, bf16[2,4096]{1,0:T(2,128)(2,1)}, bf16[2,4096]{1,0:T(2,128)(2,1)}, bf16[128,2048]{1,0:T(8,1...) custom-call(s32[1]{0:T(128)S(6)} %copy.20.lengths, s32[2]{0:T(128)} %positive_in.1, ...), custom_call_target="tpu_custom_call" | custom-call | tf_op jit(solution)/shard_map/pallas_call | solution.py:734
  79.5 2.1 %shard_map.180 = (f32[1,1]{1,0:T(1,128)}, f32[1,128]{1,0:T(1,128)}, f32[1,128]{1,0:T(1,128)}, bf16[2,4096]{1,0:T(2,128)(2,1)}, bf16[2,4096]{1,0:T(2,128)(2,1)}, ...) custom-call(f32[1,128]{1,0:T(1,128)} %get-tuple-element.23.loss, ...), custom_call_target="tpu_custom_call" | custom-call | tf_op jit(solution)/shard_map/pallas_call | solution.py:809

commit v12 on v11

--- a/solution.py
+++ b/solution.py
@@ -287,6 +287,7 @@
 
     others(lambda p: tile_copy(p).start(), j)
     x_copies(1, lambda copy: copy.start())
+    head_send("grad", grad_stage, grad_h)
 
     def half_of(core):
         return pl.ds(pl.multiple_of(16 * core, 16), 16)
@@ -298,7 +299,6 @@
 
     others(lambda p: part_copy(p).start(), d)
     q_part[d, half_of(c)] = q_cols[d, half_of(c)]
-    head_send("grad", grad_stage, grad_h)
     lane = lax.broadcasted_iota(jnp.int32, (pairs, 128), 1)
     line = lax.broadcasted_iota(jnp.int32, (pairs, 128), 0)
     real = (lane >> 5) == (line >> 3)

time: 81.9 us -> 81.9 us (level)
  no operation moved by 1% of the time
where the time goes in v12:
time: 81.9 us; the launch traced here: 81.6 us
  Pallas kernels  80.4 us (98%)
  between operations  1.29 us (2%)
    pallas_call x1, Pallas kernels, shards(): pl.pallas_call(whole, out_shape=[out((1, 128), f32), out((2, 128), f32)]...  78.3 us
    pallas_call x1, Pallas kernels, shards(): pl.pallas_call(finish, out_shape=[out((1, 1), f32), out((1, 128), f32), o...  2.1 us

profile of v12, /device:TPU:1, one launch (start us, length us, event | category | flops | bytes accessed | tf_op | source)
XLA Modules:
  0.0 81.6 jit_solution(17660932934951100545)
XLA Ops:
  1.3 78.3 %shard_map.179 = (f32[1,128]{1,0:T(1,128)}, f32[2,128]{1,0:T(2,128)}, bf16[2,4096]{1,0:T(2,128)(2,1)}, bf16[2,4096]{1,0:T(2,128)(2,1)}, bf16[128,2048]{1,0:T(8,1...) custom-call(s32[1]{0:T(128)S(6)} %copy.20.lengths, s32[2]{0:T(128)} %positive_in.1, ...), custom_call_target="tpu_custom_call" | custom-call | tf_op jit(solution)/shard_map/pallas_call | solution.py:734
  79.5 2.1 %shard_map.180 = (f32[1,1]{1,0:T(1,128)}, f32[1,128]{1,0:T(1,128)}, f32[1,128]{1,0:T(1,128)}, bf16[2,4096]{1,0:T(2,128)(2,1)}, bf16[2,4096]{1,0:T(2,128)(2,1)}, ...) custom-call(f32[1,128]{1,0:T(1,128)} %get-tuple-element.23.loss, ...), custom_call_target="tpu_custom_call" | custom-call | tf_op jit(solution)/shard_map/pallas_call | solution.py:809
